TPU v7x, 32 devices: a whole 2x2x4 slice. The times are simulated.
32 devices in a mesh: section: 4 (over y, core), expert: 8 (over z, x).
Axes of the slice: x: 2, y: 2, z: 4, core: 2. Of those that a mesh axis runs over, the one named last changes fastest.
Arguments:
- pending: bfloat16 [2, 4, 512, 3584], P(None, 'section', 'expert'), may hold values from -6 to 6
- routes: int32 [2, 4, 512, 1], P(None, 'section', 'expert'), may hold values from 0 to 3; in each aligned block of 64 rows (0 to 63, 64 to 127, ..., all dimensions but the last counted through in order) at most 16 rows name the same one
- probs: bfloat16 [2, 4, 512], P(None, 'section', 'expert'), may hold values from 0.049804688 to 0.94921875
- saved_gate: bfloat16 [2, 4, 8, 8, 16, 128], P(None, 'section', 'expert'), may hold values from -6 to 6
- saved_up: bfloat16 [2, 4, 8, 8, 16, 128], P(None, 'section', 'expert'), may hold values from -6 to 6
- w_gate: bfloat16 [4, 3584, 1024], P('section', None, 'expert'), may hold values from -0.09375 to 0.09375
- w_up: bfloat16 [4, 3584, 1024], P('section', None, 'expert'), may hold values from -0.09375 to 0.09375
- w_down: bfloat16 [4, 1024, 3584], P('section', 'expert'), may hold values from -0.09375 to 0.09375
- w_router: float32 [4, 3584, 4], P('section'), may hold values from -0.2 to 0.2
Outputs:
- passed: bfloat16 [2, 4, 512, 3584], P(None, 'section', 'expert')
Inputs may be any that keep to these rules, and one draw needn't show every extreme that they name: `routes`: among the 64 tokens of one device, at one section and direction, each expert is chosen by exactly 16 tokens.
All inputs are finite; a program needn't handle non-finite values.
Results may differ from a plain program's by a relative error of at most 0.0031.
Values may be sent and summed in bfloat16 or wider, within the bound.
A program may use at most 64 MiB of HBM per device.

v0:
```python
import jax
import jax.numpy as jnp
from jax import lax
from jax.sharding import PartitionSpec as P


def shifted(value, axis, steps):
    count = lax.axis_size(axis)
    pairs = [(source, (source + steps) % count) for source in range(count)]
    return lax.ppermute(value, axis, pairs)


def slot_tables(expert_ids, experts, capacity):
    onehot = (expert_ids[:, None] == jnp.arange(experts, dtype=jnp.int32)[None, :]).astype(
        jnp.int32
    )
    slot_index = jnp.sum((jnp.cumsum(onehot, axis=0) - 1) * onehot, axis=1)
    dest_code = expert_ids * capacity + slot_index
    selection = dest_code[:, None] == jnp.arange(experts * capacity, dtype=jnp.int32)[None, :]
    return (selection, onehot)


def outgoing(grad_in, prob, selection, experts, group, capacity):
    width = grad_in.shape[1]
    picked = lax.dot_general(
        selection.astype(jnp.bfloat16),
        grad_in,
        (((0,), (0,)), ((), ())),
        preferred_element_type=jnp.float32,
    ).astype(jnp.bfloat16)
    picked = jnp.broadcast_to(
        picked.reshape(experts, 1, capacity, width), (experts, group, capacity, width)
    )
    prob_slot = lax.dot_general(
        selection.astype(jnp.bfloat16),
        prob.reshape(-1, 1),
        (((0,), (0,)), ((), ())),
        preferred_element_type=jnp.float32,
    ).astype(jnp.bfloat16)
    prob_slot = jnp.broadcast_to(
        prob_slot.reshape(experts, 1, capacity), (experts, group, capacity)
    )
    return (
        picked.reshape(experts * group, capacity, width),
        prob_slot.reshape(experts * group, capacity),
    )


def expert_back(received, got_prob, gate_pre, up_pre, w_gate_dev, w_up_dev, w_down_dev):
    members, capacity, width = received.shape
    flat_rows = received.reshape(members * capacity, width)
    grad_z = lax.dot_general(
        flat_rows, w_down_dev, (((1,), (1,)), ((), ())), preferred_element_type=jnp.float32
    )
    gate_f = gate_pre.reshape(members * capacity, -1).astype(jnp.float32)
    up_f = up_pre.reshape(members * capacity, -1).astype(jnp.float32)
    sig = jax.nn.sigmoid(gate_f)
    hidden = gate_f * sig * up_f
    dots = jnp.sum(hidden * grad_z, axis=1).astype(jnp.bfloat16)
    grad_h = got_prob.reshape(-1).astype(jnp.float32)[:, None] * grad_z
    grad_gate = (grad_h * up_f * sig * (1.0 + gate_f * (1.0 - sig))).astype(jnp.bfloat16)
    grad_up = (grad_h * gate_f * sig).astype(jnp.bfloat16)
    parts = lax.dot_general(
        grad_gate, w_gate_dev, (((1,), (1,)), ((), ())), preferred_element_type=jnp.float32
    )
    parts = parts + lax.dot_general(
        grad_up, w_up_dev, (((1,), (1,)), ((), ())), preferred_element_type=jnp.float32
    )
    return (
        parts.astype(jnp.bfloat16).reshape(members, capacity, width),
        dots.reshape(members, capacity),
    )


def finish(parts, dots, selection, onehot, grad_in, prob, w_router_dev, experts, group, capacity):
    width = grad_in.shape[1]
    summed = jnp.sum(parts.reshape(experts, group, capacity, width).astype(jnp.float32), axis=1)
    dot_total = jnp.sum(dots.reshape(experts, group, capacity).astype(jnp.float32), axis=1)
    select_f = selection.astype(jnp.float32)
    back = jnp.dot(
        select_f, summed.reshape(experts * capacity, width), precision=lax.Precision.HIGHEST
    )
    dot_tok = jnp.dot(select_f, dot_total.reshape(-1), precision=lax.Precision.HIGHEST)
    prob_f = prob.astype(jnp.float32)
    scaled = dot_tok * prob_f * (1.0 - prob_f)
    router_term = jnp.dot(
        onehot.astype(jnp.float32) * scaled[:, None],
        jnp.transpose(w_router_dev),
        precision=lax.Precision.HIGHEST,
    )
    return (grad_in.astype(jnp.float32) + back + router_term).astype(jnp.bfloat16)


def per_device(pending, routes, probs, saved_gate, saved_up, w_gate, w_up, w_down, w_router):
    members = lax.axis_size("expert")
    experts = w_router.shape[2]
    group = members // experts
    tok_count = pending.shape[2]
    capacity = tok_count // experts
    from_above = shifted(pending[0, 0], "section", -1)
    from_below = shifted(pending[1, 0], "section", 1)
    incoming = (from_above, from_below)
    w_gate_dev = w_gate[0]
    w_up_dev = w_up[0]
    w_down_dev = w_down[0]
    w_router_dev = w_router[0]
    tables = [slot_tables(routes[direction, 0, :, 0], experts, capacity) for direction in range(2)]
    sends = [
        outgoing(
            incoming[direction], probs[direction, 0], tables[direction][0], experts, group, capacity
        )
        for direction in range(2)
    ]
    results = []
    for direction in range(2):
        received = lax.all_to_all(
            sends[direction][0], "expert", split_axis=0, concat_axis=0, tiled=True
        )
        got_prob = lax.all_to_all(
            sends[direction][1], "expert", split_axis=0, concat_axis=0, tiled=True
        )
        parts, dots = expert_back(
            received,
            got_prob,
            saved_gate[direction, 0, 0],
            saved_up[direction, 0, 0],
            w_gate_dev,
            w_up_dev,
            w_down_dev,
        )
        parts, dots = (
            lax.all_to_all(parts, "expert", split_axis=0, concat_axis=0, tiled=True),
            lax.all_to_all(dots, "expert", split_axis=0, concat_axis=0, tiled=True),
        )
        results.append(
            finish(
                parts,
                dots,
                tables[direction][0],
                tables[direction][1],
                incoming[direction],
                probs[direction, 0],
                w_router_dev,
                experts,
                group,
                capacity,
            )
        )
    return jnp.stack(results)[:, None]


def solution(mesh):
    in_specs = (
        P(None, "section", "expert", None),
        P(None, "section", "expert", None),
        P(None, "section", "expert"),
        P(None, "section", "expert", None, None, None),
        P(None, "section", "expert", None, None, None),
        P("section", None, "expert"),
        P("section", None, "expert"),
        P("section", "expert", None),
        P("section", None, None),
    )
    out_specs = P(None, "section", "expert", None)
    return jax.shard_map(
        per_device, mesh=mesh, in_specs=in_specs, out_specs=out_specs, check_vma=False
    )
```

profile of v0, /device:TPU:0, one launch (start us, length us, event | category | flops | bytes accessed | tf_op | source)
XLA Modules:
  0.0 152.4 jit_solution(677644253895521763)
XLA Ops:
  0.0 1.3 slice_bitcast_fusion.1
  1.3 2.5 %collective-permute-start = (bf16[64,3584]{1,0:T(8,128)(2,1)S(1)}, bf16[64,3584]{1,0:T(8,128)(2,1)S(1)}, u32[]{:S(2)}, u32[]{:S(2)}) collective-permute-start(bf16[64,3584]{1,0:T(8,128)(2,1)S(1)} %get-tuple-element.5), channel_id=1, source_target_pairs={{0,24},{8,0},{16,8},{24,16},{1,25},{9,1},{17,9},{25,17},{2,26},{10... | collective-permute-start | bytes 1376264 | tf_op jit(solution)/shard_map/ppermute | solution.py:10
  4.6 0.6 copy.28
  5.2 5.8 %all-to-all-start = ((bf16[8,1,16]{2,1,0:T(2,128)(2,1)}), bf16[8,1,16]{2,1,0:T(2,128)(2,1)S(1)}, u32[]{:S(2)}, u32[]{:S(2)}) async-start(bf16[8,1,16]{2,1,0:T(2,128)(2,1)} %copy.28), calls=%async_computation | async-start | bytes 8192 | tf_op jit(solution)/shard_map/all_to_all | solution.py:119
  11.9 5.6 %all-to-all-done = bf16[8,1,16]{2,1,0:T(2,128)(2,1)S(1)} async-done(((bf16[8,1,16]{2,1,0:T(2,128)(2,1)}), bf16[8,1,16]{2,1,0:T(2,128)(2,1)S(1)}, u32[]{:S(2)}, u32[]{:S(2)}) %all-to-all-start) | async-done | bytes 288 | tf_op jit(solution)/shard_map/all_to_all | solution.py:119
  17.5 3.3 %all-to-all-start.4 = ((bf16[8,1,16]{2,1,0:T(2,128)(2,1)}), bf16[8,1,16]{2,1,0:T(2,128)(2,1)S(1)}, u32[]{:S(2)}, u32[]{:S(2)}) async-start(bf16[8,1,16]{2,1,0:T(2,128)(2,1)} %copy.37), calls=%async_computation.4 | async-start | bytes 8192 | tf_op jit(solution)/shard_map/all_to_all | solution.py:119
  21.3 5.9 %all-to-all-done.4 = bf16[8,1,16]{2,1,0:T(2,128)(2,1)S(1)} async-done(((bf16[8,1,16]{2,1,0:T(2,128)(2,1)}), bf16[8,1,16]{2,1,0:T(2,128)(2,1)S(1)}, u32[]{:S(2)}, u32[]{:S(2)}) %all-to-all-start.4) | async-done | bytes 288 | tf_op jit(solution)/shard_map/all_to_all | solution.py:119
  27.2 1.0 broadcast_in_dim.21
  28.1 3.6 %all-to-all-start.1 = ((bf16[8,16,3584]{2,1,0:T(8,128)(2,1)}), bf16[8,16,3584]{2,1,0:T(8,128)(2,1)S(1)}, u32[]{:S(2)}, u32[]{:S(2)}) async-start(bf16[8,16,3584]{2,1,0:T(8,128)(2,1)} %bitcast.7), calls=%async_computation.1 | async-start | bytes 1835008 | tf_op jit(solution)/shard_map/all_to_all | solution.py:116
  31.8 7.9 %collective-permute-done.1 = bf16[64,3584]{1,0:T(8,128)(2,1)S(1)} collective-permute-done((bf16[64,3584]{1,0:T(8,128)(2,1)S(1)}, bf16[64,3584]{1,0:T(8,128)(2,1)S(1)}, u32[]{:S(2)}, u32[]{:S(2)}) %collective-permute-start.1) | collective-permute-done | bytes 458784 | tf_op jit(solution)/shard_map/ppermute | solution.py:10
  39.7 1.2 convolution_convert_fusion
  40.8 11.3 %all-to-all-done.1 = bf16[8,16,3584]{2,1,0:T(8,128)(2,1)S(1)} async-done(((bf16[8,16,3584]{2,1,0:T(8,128)(2,1)}), bf16[8,16,3584]{2,1,0:T(8,128)(2,1)S(1)}, u32[]{:S(2)}, u32[]{:S(2)}) %all-to-all-start.1) | async-done | bytes 917536 | tf_op jit(solution)/shard_map/all_to_all | solution.py:116
  52.2 2.1 %broadcast_in_dim.48 = bf16[4,2,16,3584]{3,2,1,0:T(8,128)(2,1)} broadcast(bf16[4,16,3584]{2,1,0:T(8,128)(2,1)} %bitcast.141), dimensions={0,2,3} | broadcast | bytes 1376256 | tf_op jit(solution)/shard_map/broadcast_in_dim | solution.py:31
  54.3 4.2 %all-to-all-start.5 = ((bf16[8,16,3584]{2,1,0:T(8,128)(2,1)}), bf16[8,16,3584]{2,1,0:T(8,128)(2,1)}, u32[]{:S(2)}, u32[]{:S(2)}) async-start(bf16[8,16,3584]{2,1,0:T(8,128)(2,1)} %bitcast.135), calls=%async_computation.5 | async-start | bytes 1835008 | tf_op jit(solution)/shard_map/all_to_all | solution.py:116
  59.5 0.7 convert_element_type.224
  60.7 19.2 %all-to-all-done.5 = bf16[8,16,3584]{2,1,0:T(8,128)(2,1)} async-done(((bf16[8,16,3584]{2,1,0:T(8,128)(2,1)}), bf16[8,16,3584]{2,1,0:T(8,128)(2,1)}, u32[]{:S(2)}, u32[]{:S(2)}) %all-to-all-start.5) | async-done | bytes 917536 | tf_op jit(solution)/shard_map/all_to_all | solution.py:116
  79.9 3.4 %all-to-all-start.3 = ((bf16[8,1,16]{2,1,0:T(2,128)(2,1)}), bf16[8,1,16]{2,1,0:T(2,128)(2,1)S(1)}, u32[]{:S(2)}, u32[]{:S(2)}) async-start(bf16[8,1,16]{2,1,0:T(2,128)(2,1)} %convert_element_type.224), calls=%async_computation.3 | async-start | bytes 8192 | tf_op jit(solution)/shard_map/all_to_all | solution.py:133
  83.3 1.9 %multiply_reduce_fusion = (bf16[128]{0:T(256)(128)(2,1)S(1)}, f32[128,128]{0,1:T(8,128)S(1)}) fusion(f32[128,128]{0,1:T(8,128)S(1)} %copy.38, f32[128,128]{0,1:T(8,128)S(1)} %copy.39, bf16[128,3584]{1,0:T(8,128)(2,1)} %bitcast.31, bf16[1,128,3584]{2,1,0:T(8,128)(2,1)} %param.16), kind=kOutput, calls=%fused_computation.35 | convolution fusion | flops 117555072 | bytes 2031872 | tf_op jit(solution)/shard_map/dot_general | solution.py:52
  85.2 0.7 convert_element_type.225
  85.9 3.9 %all-to-all-done.3 = bf16[8,1,16]{2,1,0:T(2,128)(2,1)S(1)} async-done(((bf16[8,1,16]{2,1,0:T(2,128)(2,1)}), bf16[8,1,16]{2,1,0:T(2,128)(2,1)S(1)}, u32[]{:S(2)}, u32[]{:S(2)}) %all-to-all-start.3) | async-done | bytes 288 | tf_op jit(solution)/shard_map/all_to_all | solution.py:133
  89.8 3.3 %all-to-all-start.7 = ((bf16[8,1,16]{2,1,0:T(2,128)(2,1)}), bf16[8,1,16]{2,1,0:T(2,128)(2,1)S(1)}, u32[]{:S(2)}, u32[]{:S(2)}) async-start(bf16[8,1,16]{2,1,0:T(2,128)(2,1)} %convert_element_type.225), calls=%async_computation.7 | async-start | bytes 8192 | tf_op jit(solution)/shard_map/all_to_all | solution.py:133
  93.1 2.6 %fusion = bf16[128,3584]{1,0:T(8,128)(2,1)} fusion(f32[128,3584]{1,0:T(8,128)S(1)} %fusion.12, bf16[1,3584,128]{2,1,0:T(8,128)(2,1)} %param.15, f32[128,128]{0,1:T(8,128)S(1)} %copy.30, f32[128,128]{0,1:T(8,128)S(1)} %get-tuple-element.18, f32[128]{0:T(128)} %copy-done.10), kind=kOutput, calls=%fused_computation.2 | convolution fusion | flops 118472704 | bytes 3801600 | tf_op jit(solution)/shard_map/dot_general | solution.py:66
  95.6 3.8 %all-to-all-done.7 = bf16[8,1,16]{2,1,0:T(2,128)(2,1)S(1)} async-done(((bf16[8,1,16]{2,1,0:T(2,128)(2,1)}), bf16[8,1,16]{2,1,0:T(2,128)(2,1)S(1)}, u32[]{:S(2)}, u32[]{:S(2)}) %all-to-all-start.7) | async-done | bytes 288 | tf_op jit(solution)/shard_map/all_to_all | solution.py:133
  99.4 3.6 %all-to-all-start.2 = ((bf16[8,16,3584]{2,1,0:T(8,128)(2,1)}), bf16[8,16,3584]{2,1,0:T(8,128)(2,1)S(1)}, u32[]{:S(2)}, u32[]{:S(2)}) async-start(bf16[8,16,3584]{2,1,0:T(8,128)(2,1)} %bitcast.139), calls=%async_computation.2 | async-start | bytes 1835008 | tf_op jit(solution)/shard_map/all_to_all | solution.py:132
  103.5 0.6 copy-done.2
  104.1 1.4 fusion.1
  105.5 17.7 %all-to-all-done.2 = bf16[8,16,3584]{2,1,0:T(8,128)(2,1)S(1)} async-done(((bf16[8,16,3584]{2,1,0:T(8,128)(2,1)}), bf16[8,16,3584]{2,1,0:T(8,128)(2,1)S(1)}, u32[]{:S(2)}, u32[]{:S(2)}) %all-to-all-start.2) | async-done | bytes 917536 | tf_op jit(solution)/shard_map/all_to_all | solution.py:132
  123.2 3.6 %all-to-all-start.6 = ((bf16[8,16,3584]{2,1,0:T(8,128)(2,1)}), bf16[8,16,3584]{2,1,0:T(8,128)(2,1)S(1)}, u32[]{:S(2)}, u32[]{:S(2)}) async-start(bf16[8,16,3584]{2,1,0:T(8,128)(2,1)} %bitcast.138), calls=%async_computation.6 | async-start | bytes 1835008 | tf_op jit(solution)/shard_map/all_to_all | solution.py:132
  128.2 20.5 %all-to-all-done.6 = bf16[8,16,3584]{2,1,0:T(8,128)(2,1)S(1)} async-done(((bf16[8,16,3584]{2,1,0:T(8,128)(2,1)}), bf16[8,16,3584]{2,1,0:T(8,128)(2,1)S(1)}, u32[]{:S(2)}, u32[]{:S(2)}) %all-to-all-start.6) | async-done | bytes 917536 | tf_op jit(solution)/shard_map/all_to_all | solution.py:132
  149.5 0.9 fusion.18
  150.4 1.0 fusion.19
  151.4 1.0 maximum_bitcast_fusion
  (81 shorter events, 6.3 us)
Async XLA Ops:
  0.0 60.2 %copy-start = (bf16[1,3584,128]{2,1,0:T(8,128)(2,1)S(1)}, bf16[1,3584,128]{2,1,0:T(8,128)(2,1)}, u32[]{:S(2)}) copy-start(bf16[1,3584,128]{2,1,0:T(8,128)(2,1)} %param.14) | copy-start | bytes 2752516
  0.0 3.8 %copy-start.15 = (s32[2,1,64,1]{2,3,1,0:T(1,128)S(1)}, s32[2,1,64,1]{2,3,1,0:T(1,128)}, u32[]{:S(2)}) copy-start(s32[2,1,64,1]{2,3,1,0:T(1,128)} %param.10) | copy-start | bytes 1540
  0.0 4.3 %copy-start.16 = (bf16[2,1,64]{2,0,1:T(2,128)(2,1)S(1)}, bf16[2,1,64]{2,0,1:T(2,128)(2,1)}, u32[]{:S(2)}) copy-start(bf16[2,1,64]{2,0,1:T(2,128)(2,1)} %param.11) | copy-start | bytes 772
  1.3 19.5 %collective-permute-start = (bf16[64,3584]{1,0:T(8,128)(2,1)S(1)}, bf16[64,3584]{1,0:T(8,128)(2,1)S(1)}, u32[]{:S(2)}, u32[]{:S(2)}) collective-permute-start(bf16[64,3584]{1,0:T(8,128)(2,1)S(1)} %get-tuple-element.5), channel_id=1, source_target_pairs={{0,24},{8,0},{16,8},{24,16},{1,25},{9,1},{17,9},{25,17},{2,26},{10... | collective-permute-start | bytes 1376264 | tf_op jit(solution)/shard_map/ppermute | solution.py:10
  3.8 17.1 %copy-start.8 = (s32[64]{0:T(128)}, s32[64]{0:T(128)S(1)}, u32[]{:S(2)}) copy-start(s32[64]{0:T(128)S(1)} %get-tuple-element.13) | copy-start | bytes 772
  4.3 23.8 %copy-start.13 = (s32[64]{0:T(128)}, s32[64]{0:T(128)S(1)}, u32[]{:S(2)}) copy-start(s32[64]{0:T(128)S(1)} %get-tuple-element.11) | copy-start | bytes 772
  4.3 35.3 %copy-start.11 = (s32[64]{0:T(128)}, s32[64]{0:T(128)S(1)}, u32[]{:S(2)}) copy-start(s32[64]{0:T(128)S(1)} %get-tuple-element.12) | copy-start | bytes 772
  5.2 12.3 %all-to-all-start = ((bf16[8,1,16]{2,1,0:T(2,128)(2,1)}), bf16[8,1,16]{2,1,0:T(2,128)(2,1)S(1)}, u32[]{:S(2)}, u32[]{:S(2)}) async-start(bf16[8,1,16]{2,1,0:T(2,128)(2,1)} %copy.28), calls=%async_computation | async-start | bytes 8192 | tf_op jit(solution)/shard_map/all_to_all | solution.py:119
  17.5 9.6 %all-to-all-start.4 = ((bf16[8,1,16]{2,1,0:T(2,128)(2,1)}), bf16[8,1,16]{2,1,0:T(2,128)(2,1)S(1)}, u32[]{:S(2)}, u32[]{:S(2)}) async-start(bf16[8,1,16]{2,1,0:T(2,128)(2,1)} %copy.37), calls=%async_computation.4 | async-start | bytes 8192 | tf_op jit(solution)/shard_map/all_to_all | solution.py:119
  21.3 10.5 %copy-start.6 = (bf16[2,1,1,8,16,128]{5,4,3,2,1,0:T(8,128)(2,1)S(1)}, bf16[2,1,1,8,16,128]{5,4,3,2,1,0:T(8,128)(2,1)}, u32[]{:S(2)}) copy-start(bf16[2,1,1,8,16,128]{5,4,3,2,1,0:T(8,128)(2,1)} %param.12) | copy-start | bytes 196612
  28.1 24.0 %all-to-all-start.1 = ((bf16[8,16,3584]{2,1,0:T(8,128)(2,1)}), bf16[8,16,3584]{2,1,0:T(8,128)(2,1)S(1)}, u32[]{:S(2)}, u32[]{:S(2)}) async-start(bf16[8,16,3584]{2,1,0:T(8,128)(2,1)} %bitcast.7), calls=%async_computation.1 | async-start | bytes 1835008 | tf_op jit(solution)/shard_map/all_to_all | solution.py:116
  31.7 8.0 %collective-permute-start.1 = (bf16[64,3584]{1,0:T(8,128)(2,1)S(1)}, bf16[64,3584]{1,0:T(8,128)(2,1)S(1)}, u32[]{:S(2)}, u32[]{:S(2)}) collective-permute-start(bf16[64,3584]{1,0:T(8,128)(2,1)S(1)} %get-tuple-element.6), channel_id=1, source_target_pairs={{0,8},{8,16},{16,24},{24,0},{1,9},{9,17},{17,25},{25,1},{2,10},{10... | collective-permute-start | bytes 1376264 | tf_op jit(solution)/shard_map/ppermute | solution.py:10
  39.7 12.5 %copy-start.3 = (bf16[64,3584]{1,0:T(8,128)(2,1)}, bf16[64,3584]{1,0:T(8,128)(2,1)S(1)}, u32[]{:S(2)}) copy-start(bf16[64,3584]{1,0:T(8,128)(2,1)S(1)} %collective-permute-done.1) | copy-start | bytes 1376260
  40.8 17.8 %copy-start.7 = (bf16[2,1,1,8,16,128]{5,4,3,2,1,0:T(8,128)(2,1)S(1)}, bf16[2,1,1,8,16,128]{5,4,3,2,1,0:T(8,128)(2,1)}, u32[]{:S(2)}) copy-start(bf16[2,1,1,8,16,128]{5,4,3,2,1,0:T(8,128)(2,1)} %param.13) | copy-start | bytes 196612
  52.2 6.9 %copy-start.1 = (bf16[1,128,3584]{2,1,0:T(8,128)(2,1)S(1)}, bf16[1,128,3584]{2,1,0:T(8,128)(2,1)}, u32[]{:S(2)}) copy-start(bf16[1,128,3584]{2,1,0:T(8,128)(2,1)} %param.16) | copy-start | bytes 2752516
  54.3 25.6 %all-to-all-start.5 = ((bf16[8,16,3584]{2,1,0:T(8,128)(2,1)}), bf16[8,16,3584]{2,1,0:T(8,128)(2,1)}, u32[]{:S(2)}, u32[]{:S(2)}) async-start(bf16[8,16,3584]{2,1,0:T(8,128)(2,1)} %bitcast.135), calls=%async_computation.5 | async-start | bytes 1835008 | tf_op jit(solution)/shard_map/all_to_all | solution.py:116
  59.1 1.6 %copy-start.10 = (f32[128]{0:T(128)}, f32[128]{0:T(128)S(1)}, u32[]{:S(2)}) copy-start(f32[128]{0:T(128)S(1)} %reshape.162) | copy-start | bytes 1540
  79.9 9.9 %all-to-all-start.3 = ((bf16[8,1,16]{2,1,0:T(2,128)(2,1)}), bf16[8,1,16]{2,1,0:T(2,128)(2,1)S(1)}, u32[]{:S(2)}, u32[]{:S(2)}) async-start(bf16[8,1,16]{2,1,0:T(2,128)(2,1)} %convert_element_type.224), calls=%async_computation.3 | async-start | bytes 8192 | tf_op jit(solution)/shard_map/all_to_all | solution.py:133
  89.8 9.6 %all-to-all-start.7 = ((bf16[8,1,16]{2,1,0:T(2,128)(2,1)}), bf16[8,1,16]{2,1,0:T(2,128)(2,1)S(1)}, u32[]{:S(2)}, u32[]{:S(2)}) async-start(bf16[8,1,16]{2,1,0:T(2,128)(2,1)} %convert_element_type.225), calls=%async_computation.7 | async-start | bytes 8192 | tf_op jit(solution)/shard_map/all_to_all | solution.py:133
  99.4 23.8 %all-to-all-start.2 = ((bf16[8,16,3584]{2,1,0:T(8,128)(2,1)}), bf16[8,16,3584]{2,1,0:T(8,128)(2,1)S(1)}, u32[]{:S(2)}, u32[]{:S(2)}) async-start(bf16[8,16,3584]{2,1,0:T(8,128)(2,1)} %bitcast.139), calls=%async_computation.2 | async-start | bytes 1835008 | tf_op jit(solution)/shard_map/all_to_all | solution.py:132
  103.0 1.2 copy-start.2
  105.5 21.5 %copy-start.14 = (s32[64]{0:T(128)S(1)}, s32[64]{0:T(128)}, u32[]{:S(2)}) copy-start(s32[64]{0:T(128)} %copy-done.13) | copy-start | bytes 772
  105.5 21.5 %copy-start.17 = (bf16[2,1,64]{2,0,1:T(2,128)(2,1)S(1)}, bf16[2,1,64]{2,0,1:T(2,128)(2,1)}, u32[]{:S(2)}) copy-start(bf16[2,1,64]{2,0,1:T(2,128)(2,1)} %param.11) | copy-start | bytes 772
  105.5 21.7 %copy-start.12 = (s32[64]{0:T(128)S(1)}, s32[64]{0:T(128)}, u32[]{:S(2)}) copy-start(s32[64]{0:T(128)} %copy-done.11) | copy-start | bytes 772
  123.2 25.5 %all-to-all-start.6 = ((bf16[8,16,3584]{2,1,0:T(8,128)(2,1)}), bf16[8,16,3584]{2,1,0:T(8,128)(2,1)S(1)}, u32[]{:S(2)}, u32[]{:S(2)}) async-start(bf16[8,16,3584]{2,1,0:T(8,128)(2,1)} %bitcast.138), calls=%async_computation.6 | async-start | bytes 1835008 | tf_op jit(solution)/shard_map/all_to_all | solution.py:132
  128.2 21.2 %copy-start.5 = (f32[1,3584,4]{1,2,0:T(4,128)S(1)}, f32[1,3584,4]{1,2,0:T(4,128)}, u32[]{:S(2)}) copy-start(f32[1,3584,4]{1,2,0:T(4,128)} %param.17) | copy-start | bytes 172036
  128.2 21.2 %copy-start.9 = (s32[64]{0:T(128)S(1)}, s32[64]{0:T(128)}, u32[]{:S(2)}) copy-start(s32[64]{0:T(128)} %copy-done.8) | copy-start | bytes 772
  148.8 1.5 %copy-start.4 = (bf16[64,3584]{1,0:T(8,128)(2,1)S(1)}, bf16[64,3584]{1,0:T(8,128)(2,1)}, u32[]{:S(2)}) copy-start(bf16[64,3584]{1,0:T(8,128)(2,1)} %copy-done.3) | copy-start | bytes 1376260
where the time goes:
time: 153 us; the launch traced here: 152 us
  waiting for transfers between devices  95.7 us (63%)
  starting transfers between devices  33.3 us (22%)
  matrix products  12.5 us (8%)
  local copies, waits for them, and re-layouts  8.54 us (6%)
  other arithmetic  1.97 us (1%)
    all_to_all x2, waiting for transfers between devices, per_device(): lax.all_to_all(parts, 'expert', split_axis=0, concat_axis=0, tiled=True)  38.2 us
    all_to_all x2, waiting for transfers between devices, per_device(): lax.all_to_all(sends[direction][0], 'expert', split_axis=0, concat_axis=0...  30.5 us
    all_to_all x2, waiting for transfers between devices, per_device(): lax.all_to_all(sends[direction][1], 'expert', split_axis=0, concat_axis=0...  11.5 us
    all_to_all x2, starting transfers between devices, per_device(): lax.all_to_all(sends[direction][1], 'expert', split_axis=0, concat_axis=0...  9.12 us
    ppermute x2, waiting for transfers between devices, shifted(): return lax.ppermute(value, axis, pairs)  7.87 us
    all_to_all x2, starting transfers between devices, per_device(): lax.all_to_all(sends[direction][0], 'expert', split_axis=0, concat_axis=0...  7.79 us
    all_to_all x2, waiting for transfers between devices, per_device(): lax.all_to_all(dots, 'expert', split_axis=0, concat_axis=0, tiled=True)  7.66 us
    all_to_all x2, starting transfers between devices, per_device(): lax.all_to_all(parts, 'expert', split_axis=0, concat_axis=0, tiled=True)  7.11 us
  transfers between devices with their start and end apart: 10, of which 9 were waited for; matrix products, arithmetic and copies ran while one was open for 9% of the time, Pallas kernels for 0%

commit v1 on v0

v1 whole, which is shorter than its diff:
```python
import functools

import jax
import jax.numpy as jnp
from jax import lax
from jax.experimental import pallas as pl
from jax.experimental.pallas import tpu as pltpu
from jax.sharding import PartitionSpec as P

MESH = pl.DeviceIdType.MESH
F32 = jnp.float32
BF16 = jnp.bfloat16
CHUNKS = 2


def dot(a, b, contract):
    return lax.dot_general(a, b, (contract, ((), ())), preferred_element_type=F32)


def layer_kernel(
    sections, experts, group, chunks,
    pend, routes, probs, gate, up, w_gate, w_up, w_down, router, out,
    grad, wgu, wd, picked, rows, p_own, p_got, parts, halves, sums, home,
    load_sem, shift_send, shift_recv, p_send, p_recv, there_send, there_recv,
    fwd_send, fwd_recv, red_send, red_recv, back_send, back_recv,
):
    members = experts * group
    tokens, width = grad.shape[1], grad.shape[2]
    cap = tokens // experts
    step = width // chunks
    cols = [pl.ds(c * step, step) for c in range(chunks)]
    sec, me = lax.axis_index("section"), lax.axis_index("expert")
    mine, side = me // group, me % group
    odd = sec % 2
    way = (odd, 1 - odd)
    source = (sec + 1 - 2 * odd, lax.rem(sec + sections - 1 + 2 * odd, sections))

    def at(expert, member):
        return (sec, expert * group + member)

    def remote(src, dst, send, recv, device):
        return pltpu.make_async_remote_copy(
            src_ref=src, dst_ref=dst, send_sem=send, recv_sem=recv,
            device_id=device, device_id_type=MESH)

    loads = [
        pltpu.make_async_copy(w_down, wd, load_sem.at[0]),
        pltpu.make_async_copy(w_gate, wgu.at[:, pl.ds(0, w_gate.shape[1])], load_sem.at[1]),
        pltpu.make_async_copy(
            w_up, wgu.at[:, pl.ds(w_gate.shape[1], w_up.shape[1])], load_sem.at[2]),
    ]
    for load in loads:
        load.start()

    barrier = pltpu.get_barrier_semaphore()
    for other in source:
        pl.semaphore_signal(barrier, inc=1, device_id=(other, me), device_id_type=MESH)
    for k in range(1, members):
        pl.semaphore_signal(
            barrier, inc=1, device_id=(sec, lax.rem(me + k, members)), device_id_type=MESH)
    pl.semaphore_wait(barrier, members + 1)

    sent = []

    def shift(f, c):
        return remote(pend.at[1 - way[f], :, cols[c]], grad.at[f, :, cols[c]],
                      shift_send.at[f, c], shift_recv.at[f, c], (source[f], me))

    for f in range(2):
        for c in range(chunks):
            copy = shift(f, c)
            copy.start()
            sent.append(copy)

    table = []
    both_routes, both_probs = routes[...], probs[...].astype(F32)
    before = (lax.broadcasted_iota(jnp.int32, (tokens, tokens), 0)
              < lax.broadcasted_iota(jnp.int32, (tokens, tokens), 1)).astype(F32)
    for f in range(2):
        swap = odd == 1
        first, second = (0, 1) if f == 0 else (1, 0)
        r = jnp.where(swap, both_routes[second:second + 1], both_routes[first:first + 1])
        p = jnp.where(swap, both_probs[second:second + 1], both_probs[first:first + 1])
        named = (lax.broadcasted_iota(jnp.int32, (8, tokens), 0) == r).astype(F32)
        count = dot(named, before, ((1,), (0,)))
        slot = jnp.sum(named * count, axis=0, keepdims=True)
        dest = r.astype(F32) * cap + slot
        select = lax.broadcasted_iota(jnp.int32, (tokens, tokens), 0).astype(F32) == dest
        table.append(select.astype(F32).astype(BF16))
        p_slot = jnp.sum(jnp.where(select, p, 0.0), axis=1, keepdims=True)
        p_own[:, f] = jnp.broadcast_to(p_slot, (tokens, 128)).astype(BF16).reshape(
            experts, cap, 128)

    def p_copy(k):
        to = lax.rem(me + k, members)
        return remote(p_own.at[to // group], p_got.at[me], p_send.at[k], p_recv.at[k], (sec, to))

    p_got[me] = p_own[mine]
    for k in range(1, members):
        copy = p_copy(k)
        copy.start()
        sent.append(copy)

    def there(f, c, k):
        to = lax.rem(mine + k, experts)
        return remote(picked.at[f, to, :, cols[c]], rows.at[f, mine, side, :, cols[c]],
                      there_send.at[f, c, k], there_recv.at[f, c, k], at(to, side))

    def forward(f, c, k, m):
        band = lax.rem(mine + experts - k, experts)
        src = picked.at[f, mine, :, cols[c]] if k == 0 else rows.at[f, band, side, :, cols[c]]
        return remote(src, rows.at[f, band, side, :, cols[c]],
                      fwd_send.at[f, c, k, m], fwd_recv.at[f, c, k, m],
                      at(mine, lax.rem(side + m, group)))

    def reduce(f, c, m):
        to = lax.rem(side + m, group)
        return remote(parts.at[f, :, to, :, cols[c]], halves.at[f, m - 1, :, :, cols[c]],
                      red_send.at[f, c, m], red_recv.at[f, c, m], at(mine, to))

    def back(f, c, k):
        to = lax.rem(mine + k, experts)
        return remote(sums.at[f, to, :, cols[c]], home.at[f, mine, :, cols[c]],
                      back_send.at[f, c, k], back_recv.at[f, c, k], at(to, side))

    def start(copy):
        copy.start()
        sent.append(copy)

    def pick(f, c):
        shift(f, c).wait_recv()
        got = dot(table[f], grad[f, :, cols[c]], ((1,), (0,))).astype(BF16)
        picked[f, :, :, cols[c]] = got.reshape(experts, cap, step)
        for k in range(experts - 1, 0, -1):
            start(there(f, c, k))
        for m in range(1, group):
            start(forward(f, c, 0, m))
        rows[f, mine, side, :, cols[c]] = picked[f, mine, :, cols[c]]

    def pass_on(f, c):
        for k in range(1, experts):
            there(f, c, k).wait_recv()
            for m in range(1, group):
                start(forward(f, c, k, m))

    def middle(f):
        z = jnp.zeros((members * cap, wd.shape[0]), F32)
        for c in range(chunks):
            for k in range(experts):
                for m in range(1, group):
                    forward(f, c, k, m).wait_recv()
            held = rows[f, :, :, :, cols[c]].reshape(members * cap, step)
            z = z + dot(held, wd[:, cols[c]], ((1,), (1,)))
        a = gate[way[f]].reshape(members * cap, -1).astype(F32)
        b = up[way[f]].reshape(members * cap, -1).astype(F32)
        p = p_got[:, f].reshape(members * cap, 128)[:, 0:1].astype(F32)
        sg = jax.nn.sigmoid(a)
        product = jnp.sum(a * sg * b * z, axis=1, keepdims=True).astype(BF16).astype(F32)
        u = p * z
        grad_gate = (u * b * sg * (1.0 + a * (1.0 - sg))).astype(BF16)
        grad_up = (u * a * sg).astype(BF16)
        hidden = jnp.concatenate([grad_gate, grad_up], axis=1)
        scaled = product * p * (1.0 - p)
        for c in range(chunks):
            column = router[pl.ds(mine, 1), cols[c]]
            part = dot(hidden, wgu[cols[c], :], ((1,), (1,))) + scaled * column
            parts[f, :, :, :, cols[c]] = part.astype(BF16).reshape(experts, group, cap, step)
            for m in range(1, group):
                start(reduce(f, c, m))

    def add_up(f, c):
        total = parts[f, :, side, :, cols[c]].astype(F32)
        for m in range(1, group):
            reduce(f, c, m).wait_recv()
            total = total + halves[f, m - 1, :, :, cols[c]].astype(F32)
        sums[f, :, :, cols[c]] = total.astype(BF16)
        for k in range(experts - 1, 0, -1):
            start(back(f, c, k))
        home[f, mine, :, cols[c]] = sums[f, mine, :, cols[c]]

    def finish(f, c):
        for k in range(1, experts):
            back(f, c, k).wait_recv()
        got = dot(table[f], home[f, :, :, cols[c]].reshape(tokens, step), ((0,), (0,)))
        out[way[f], :, cols[c]] = (grad[f, :, cols[c]].astype(F32) + got).astype(BF16)

    for c in range(chunks):
        pick(0, c)
    for c in range(chunks):
        pass_on(0, c)
        pick(1, c)
    for load in loads:
        load.wait()
    for k in range(1, members):
        p_copy(k).wait_recv()
    middle(0)
    for c in range(chunks):
        pass_on(1, c)
    for c in range(chunks):
        add_up(0, c)
    middle(1)
    for c in range(chunks):
        add_up(1, c)
    for f in range(2):
        for c in range(chunks):
            finish(f, c)
    for copy in sent:
        copy.wait_send()


def per_device(pending, routes, probs, saved_gate, saved_up, w_gate, w_up, w_down, w_router):
    sections, members = lax.axis_size("section"), lax.axis_size("expert")
    experts = w_router.shape[2]
    group = members // experts
    tokens, width = pending.shape[2], pending.shape[3]
    cap = tokens // experts
    hidden = w_gate.shape[2]
    chunks = CHUNKS
    dma, vmem = pltpu.SemaphoreType.DMA, pltpu.VMEM
    any_spec = pl.BlockSpec(memory_space=pl.ANY)
    vmem_spec = pl.BlockSpec(memory_space=pltpu.VMEM)
    result = pl.pallas_call(
        functools.partial(layer_kernel, sections, experts, group, chunks),
        out_shape=jax.ShapeDtypeStruct((2, tokens, width), BF16),
        in_specs=[any_spec] + [vmem_spec] * 4 + [any_spec] * 3 + [vmem_spec],
        out_specs=vmem_spec,
        scratch_shapes=[
            vmem((2, tokens, width), BF16),
            vmem((width, 2 * hidden), BF16),
            vmem((hidden, width), BF16),
            vmem((2, experts, cap, width), BF16),
            vmem((2, experts, group, cap, width), BF16),
            vmem((experts, 2, cap, 128), BF16),
            vmem((members, 2, cap, 128), BF16),
            vmem((2, experts, group, cap, width), BF16),
            vmem((2, max(group - 1, 1), experts, cap, width), BF16),
            vmem((2, experts, cap, width), BF16),
            vmem((2, experts, cap, width), BF16),
            dma((3,)),
            dma((2, chunks)), dma((2, chunks)),
            dma((members,)), dma((members,)),
            dma((2, chunks, experts)), dma((2, chunks, experts)),
            dma((2, chunks, experts, group)), dma((2, chunks, experts, group)),
            dma((2, chunks, group)), dma((2, chunks, group)),
            dma((2, chunks, experts)), dma((2, chunks, experts)),
        ],
        compiler_params=pltpu.CompilerParams(
            collective_id=0, has_side_effects=True, vmem_limit_bytes=56 << 20),
        cost_estimate=pl.CostEstimate(
            flops=12 * members * cap * hidden * width, bytes_accessed=8 << 20, transcendentals=0),
    )(
        pending[:, 0], routes[:, 0, :, 0], probs[:, 0], saved_gate[:, 0, 0], saved_up[:, 0, 0],
        w_gate[0], w_up[0], w_down[0], jnp.transpose(w_router[0]),
    )
    return result[:, None]


def solution(mesh):
    in_specs = (
        P(None, "section", "expert", None),
        P(None, "section", "expert", None),
        P(None, "section", "expert"),
        P(None, "section", "expert", None, None, None),
        P(None, "section", "expert", None, None, None),
        P("section", None, "expert"),
        P("section", None, "expert"),
        P("section", "expert", None),
        P("section", None, None),
    )
    out_specs = P(None, "section", "expert", None)
    return jax.shard_map(
        per_device, mesh=mesh, in_specs=in_specs, out_specs=out_specs, check_vma=False
    )
```

time: 153 us -> 72 us (0.47)
  waiting for transfers between devices: 95.7 us -> 0 us
  Pallas kernels: 0 us -> 69.6 us
  starting transfers between devices: 33.3 us -> 0 us
  matrix products: 12.5 us -> 0 us
  local copies, waits for them, and re-layouts: 8.54 us -> 2.16 us
  other arithmetic: 1.97 us -> 0 us
    all_to_all x8 -> x0, waiting for transfers between devices: 87.8 us -> none  [the longest x2 38.2 us: per_device(): lax.all_to_all(parts, 'expert', split_axis=0, concat_axis=0, tiled=True)]
    pallas_call x0 -> x1, Pallas kernels: none -> 69.6 us  [per_device(): pl.pallas_call(functools.partial(layer_kernel, sections, experts, group,...]
    all_to_all x8 -> x0, starting transfers between devices: 30.7 us -> none  [the longest x2 9.12 us: per_device(): lax.all_to_all(sends[direction][1], 'expert', split_axis=0, concat_axis=0...]
    dot_general x16 -> x0, matrix products: 12.5 us -> none  [the longest x2 3.95 us: expert_back(): lax.dot_general(grad_up, w_up_dev, (((1,), (1,)), ((), ())), preferred_el...]
    ppermute x2 -> x0, waiting for transfers between devices: 7.87 us -> none  [shifted(): return lax.ppermute(value, axis, pairs)]
    broadcast_in_dim x6 -> x0, local copies, waits for them, and re-layouts: 3.26 us -> none  [the longest x2 3.07 us: outgoing(): jnp.broadcast_to(picked.reshape(experts, 1, capacity, width), (experts, g...]
    ppermute x2 -> x0, starting transfers between devices: 2.52 us -> none  [shifted(): return lax.ppermute(value, axis, pairs)]
    convert_element_type x8 -> x0, local copies, waits for them, and re-layouts: 1.89 us -> none  [the longest x2 1.38 us: expert_back(): dots = jnp.sum(hidden * grad_z, axis=1).astype(jnp.bfloat16)]
  transfers between devices with their start and end apart: 10 -> 0, of which waited for: 9 -> 0; matrix products, arithmetic and copies ran while one was open for 9% -> 0% of each run, Pallas kernels for 0% -> 0%
where the time goes in v1:
time: 72 us; the launch traced here: 71.8 us
  Pallas kernels  69.6 us (97%)
  local copies, waits for them, and re-layouts  2.16 us (3%)
    pallas_call x1, Pallas kernels, per_device(): pl.pallas_call(functools.partial(layer_kernel, sections, experts, group,...  69.6 us
    unnamed x1, local copies, waits for them, and re-layouts  2.16 us

profile of v1, /device:TPU:0, one launch (start us, length us, event | category | flops | bytes accessed | tf_op | source)
XLA Modules:
  0.0 71.8 jit_solution(11655215017295863071)
XLA Ops:
  0.0 69.6 %shard_map.91 = bf16[2,64,3584]{2,1,0:T(8,128)(2,1)} custom-call(bf16[2,64,3584]{2,1,0:T(8,128)(2,1)} %bitcast.15, s32[2,64]{1,0:T(2,128)} %bitcast.22, bf16[2,64]{1,0:T(2,128)(2,1)} %bitcast.23, bf16[2,8,16,128]{3,2,1,0:T(8,128)(2,1)} %bitcast.19, bf16[2,8,16,128]{3,2,1,0:T(8,128)(2,1)} %bitcast.20, bf16[3584,128]{1,0:T(8,128)(2,1)} %bitcast.16, ...), custom_call_target="tpu_custom_call" | custom-call | flops 704643072 | bytes 8388608 | tf_op jit(solution)/shard_map/pallas_call | solution.py:222
  69.6 2.2 %copy.12 = bf16[2,1,64,3584]{3,2,1,0:T(8,128)(2,1)} copy(bf16[2,1,64,3584]{3,2,1,0:T(8,128)(2,1)} %bitcast.14) | data formatting | bytes 1835008

commit v2 on v1

--- a/solution.py
+++ b/solution.py
@@ -10,7 +10,7 @@
 MESH = pl.DeviceIdType.MESH
 F32 = jnp.float32
 BF16 = jnp.bfloat16
-CHUNKS = 2
+CHUNKS = 4
 
 
 def dot(a, b, contract):
@@ -20,8 +20,8 @@
 def layer_kernel(
     sections, experts, group, chunks,
     pend, routes, probs, gate, up, w_gate, w_up, w_down, router, out,
-    grad, wgu, wd, picked, rows, p_own, p_got, parts, halves, sums, home,
-    load_sem, shift_send, shift_recv, p_send, p_recv, there_send, there_recv,
+    grad, wgu, wd, picked, rows, p_own, p_got, parts, halves, sums, home, done,
+    load_sem, out_sem, shift_send, shift_recv, p_send, p_recv, there_send, there_recv,
     fwd_send, fwd_recv, red_send, red_recv, back_send, back_recv,
 ):
     members = experts * group
@@ -143,14 +143,14 @@
             for m in range(1, group):
                 start(forward(f, c, k, m))
 
-    def middle(f):
-        z = jnp.zeros((members * cap, wd.shape[0]), F32)
-        for c in range(chunks):
-            for k in range(experts):
-                for m in range(1, group):
-                    forward(f, c, k, m).wait_recv()
-            held = rows[f, :, :, :, cols[c]].reshape(members * cap, step)
-            z = z + dot(held, wd[:, cols[c]], ((1,), (1,)))
+    def inner(f, c, z):
+        for k in range(experts):
+            for m in range(1, group):
+                forward(f, c, k, m).wait_recv()
+        held = rows[f, :, :, :, cols[c]].reshape(members * cap, step)
+        return z + dot(held, wd[:, cols[c]], ((1,), (1,)))
+
+    def middle(f, z):
         a = gate[way[f]].reshape(members * cap, -1).astype(F32)
         b = up[way[f]].reshape(members * cap, -1).astype(F32)
         p = p_got[:, f].reshape(members * cap, 128)[:, 0:1].astype(F32)
@@ -160,13 +160,14 @@
         grad_gate = (u * b * sg * (1.0 + a * (1.0 - sg))).astype(BF16)
         grad_up = (u * a * sg).astype(BF16)
         hidden = jnp.concatenate([grad_gate, grad_up], axis=1)
-        scaled = product * p * (1.0 - p)
-        for c in range(chunks):
-            column = router[pl.ds(mine, 1), cols[c]]
-            part = dot(hidden, wgu[cols[c], :], ((1,), (1,))) + scaled * column
-            parts[f, :, :, :, cols[c]] = part.astype(BF16).reshape(experts, group, cap, step)
-            for m in range(1, group):
-                start(reduce(f, c, m))
+        return hidden, product * p * (1.0 - p)
+
+    def outer(f, c, hidden, scaled):
+        column = router[pl.ds(mine, 1), cols[c]]
+        part = dot(hidden, wgu[cols[c], :], ((1,), (1,))) + scaled * column
+        parts[f, :, :, :, cols[c]] = part.astype(BF16).reshape(experts, group, cap, step)
+        for m in range(1, group):
+            start(reduce(f, c, m))
 
     def add_up(f, c):
         total = parts[f, :, side, :, cols[c]].astype(F32)
@@ -182,30 +183,62 @@
         for k in range(1, experts):
             back(f, c, k).wait_recv()
         got = dot(table[f], home[f, :, :, cols[c]].reshape(tokens, step), ((0,), (0,)))
-        out[way[f], :, cols[c]] = (grad[f, :, cols[c]].astype(F32) + got).astype(BF16)
-
+        done[f, :, cols[c]] = (grad[f, :, cols[c]].astype(F32) + got).astype(BF16)
+        copy = pltpu.make_async_copy(
+            done.at[f, :, cols[c]], out.at[way[f], :, cols[c]], out_sem.at[f, c])
+        copy.start()
+        written.append(copy)
+
+    written = []
     for c in range(chunks):
         pick(0, c)
+    zero = jnp.zeros((members * cap, wd.shape[0]), F32)
+    loads[0].wait()
+    z = zero
     for c in range(chunks):
         pass_on(0, c)
         pick(1, c)
-    for load in loads:
-        load.wait()
+        if c > 0:
+            z = inner(0, c - 1, z)
+    z = inner(0, chunks - 1, z)
     for k in range(1, members):
         p_copy(k).wait_recv()
-    middle(0)
+    hidden = middle(0, z)
+    for load in loads[1:]:
+        load.wait()
+    for c in range(chunks):
+        outer(0, c, *hidden)
+    z = zero
     for c in range(chunks):
         pass_on(1, c)
-    for c in range(chunks):
         add_up(0, c)
-    middle(1)
-    for c in range(chunks):
+        if c > 0:
+            z = inner(1, c - 1, z)
+    z = inner(1, chunks - 1, z)
+    hidden = middle(1, z)
+    for c in range(chunks):
+        outer(1, c, *hidden)
+    for c in range(chunks):
+        finish(0, c)
         add_up(1, c)
-    for f in range(2):
-        for c in range(chunks):
-            finish(f, c)
+    for c in range(chunks):
+        finish(1, c)
     for copy in sent:
         copy.wait_send()
+    for copy in written:
+        copy.wait()
+
+
+def copy_kernel(src, dst, sem):
+    copies = [
+        pltpu.make_async_copy(src.at[i, pl.ds(r, 16)], dst.at[i, pl.ds(r, 16)], sem.at[i, r // 16])
+        for i in range(src.shape[0])
+        for r in range(0, src.shape[1], 16)
+    ]
+    for copy in copies:
+        copy.start()
+    for copy in copies:
+        copy.wait()
 
 
 def per_device(pending, routes, probs, saved_gate, saved_up, w_gate, w_up, w_down, w_router):
@@ -223,7 +256,7 @@
         functools.partial(layer_kernel, sections, experts, group, chunks),
         out_shape=jax.ShapeDtypeStruct((2, tokens, width), BF16),
         in_specs=[any_spec] + [vmem_spec] * 4 + [any_spec] * 3 + [vmem_spec],
-        out_specs=vmem_spec,
+        out_specs=any_spec,
         scratch_shapes=[
             vmem((2, tokens, width), BF16),
             vmem((width, 2 * hidden), BF16),
@@ -236,7 +269,9 @@
             vmem((2, max(group - 1, 1), experts, cap, width), BF16),
             vmem((2, experts, cap, width), BF16),
             vmem((2, experts, cap, width), BF16),
+            vmem((2, tokens, width), BF16),
             dma((3,)),
+            dma((2, chunks)),
             dma((2, chunks)), dma((2, chunks)),
             dma((members,)), dma((members,)),
             dma((2, chunks, experts)), dma((2, chunks, experts)),
@@ -252,6 +287,13 @@
         pending[:, 0], routes[:, 0, :, 0], probs[:, 0], saved_gate[:, 0, 0], saved_up[:, 0, 0],
         w_gate[0], w_up[0], w_down[0], jnp.transpose(w_router[0]),
     )
+    result = pl.pallas_call(
+        copy_kernel,
+        out_shape=jax.ShapeDtypeStruct(result.shape, BF16),
+        in_specs=[any_spec],
+        out_specs=any_spec,
+        scratch_shapes=[dma((2, tokens // 16))],
+    )(result)
     return result[:, None]
 
 

time: 72 us -> 95.7 us (1.33)
  Pallas kernels: 69.6 us -> 95.6 us
  local copies, waits for them, and re-layouts: 2.16 us -> 0 us
    pallas_call x0 -> x1, Pallas kernels: none -> 29 us  [per_device(): pl.pallas_call(copy_kernel, out_shape=jax.ShapeDtypeStruct(result.shape,...]
    pallas_call x1, Pallas kernels: 69.6 us -> 66.6 us  [per_device(): pl.pallas_call(functools.partial(layer_kernel, sections, experts, group,...]
    unnamed x1 -> x0, local copies, waits for them, and re-layouts: 2.16 us -> none
where the time goes in v2:
time: 95.7 us; the launch traced here: 95.6 us
  Pallas kernels  95.6 us (100%)
    pallas_call x1, Pallas kernels, per_device(): pl.pallas_call(functools.partial(layer_kernel, sections, experts, group,...  66.6 us
    pallas_call x1, Pallas kernels, per_device(): pl.pallas_call(copy_kernel, out_shape=jax.ShapeDtypeStruct(result.shape,...  29 us

profile of v2, /device:TPU:0, one launch (start us, length us, event | category | flops | bytes accessed | tf_op | source)
XLA Modules:
  0.0 95.6 jit_solution(3090347992831015446)
XLA Ops:
  0.0 66.6 %shard_map.91.src = bf16[2,64,3584]{2,1,0:T(8,128)(2,1)} custom-call(bf16[2,64,3584]{2,1,0:T(8,128)(2,1)} %bitcast.14, s32[2,64]{1,0:T(2,128)} %bitcast.21, bf16[2,64]{1,0:T(2,128)(2,1)} %bitcast.22, bf16[2,8,16,128]{3,2,1,0:T(8,128)(2,1)} %bitcast.18, bf16[2,8,16,128]{3,2,1,0:T(8,128)(2,1)} %bitcast.19, bf16[3584,128]{1,0:T(8,128)(2,1)} %bitcast.15, ...), custom_call_target="tpu_custom_call" | custom-call | flops 704643072 | bytes 8388608 | tf_op jit(solution)/shard_map/pallas_call | solution.py:255
  66.6 29.0 %shard_map.92 = bf16[2,64,3584]{2,1,0:T(8,128)(2,1)} custom-call(bf16[2,64,3584]{2,1,0:T(8,128)(2,1)} %shard_map.91.src), custom_call_target="tpu_custom_call" | custom-call | tf_op jit(solution)/shard_map/pallas_call | solution.py:290

commit v3 on v2

--- a/solution.py
+++ b/solution.py
@@ -20,8 +20,8 @@
 def layer_kernel(
     sections, experts, group, chunks,
     pend, routes, probs, gate, up, w_gate, w_up, w_down, router, out,
-    grad, wgu, wd, picked, rows, p_own, p_got, parts, halves, sums, home, done,
-    load_sem, out_sem, shift_send, shift_recv, p_send, p_recv, there_send, there_recv,
+    grad, wgu, wd, picked, rows, p_own, p_got, parts, halves, sums, home, done, held,
+    stage_sem, load_sem, out_sem, shift_send, shift_recv, p_send, p_recv, there_send, there_recv,
     fwd_send, fwd_recv, red_send, red_recv, back_send, back_recv,
 ):
     members = experts * group
@@ -43,13 +43,16 @@
             src_ref=src, dst_ref=dst, send_sem=send, recv_sem=recv,
             device_id=device, device_id_type=MESH)
 
+    stage = [
+        pltpu.make_async_copy(pend.at[1 - way[f]], held.at[f], stage_sem.at[f]) for f in range(2)
+    ]
     loads = [
         pltpu.make_async_copy(w_down, wd, load_sem.at[0]),
         pltpu.make_async_copy(w_gate, wgu.at[:, pl.ds(0, w_gate.shape[1])], load_sem.at[1]),
         pltpu.make_async_copy(
             w_up, wgu.at[:, pl.ds(w_gate.shape[1], w_up.shape[1])], load_sem.at[2]),
     ]
-    for load in loads:
+    for load in stage + loads:
         load.start()
 
     barrier = pltpu.get_barrier_semaphore()
@@ -63,10 +66,11 @@
     sent = []
 
     def shift(f, c):
-        return remote(pend.at[1 - way[f], :, cols[c]], grad.at[f, :, cols[c]],
+        return remote(held.at[f, :, cols[c]], grad.at[f, :, cols[c]],
                       shift_send.at[f, c], shift_recv.at[f, c], (source[f], me))
 
     for f in range(2):
+        stage[f].wait()
         for c in range(chunks):
             copy = shift(f, c)
             copy.start()
@@ -229,16 +233,8 @@
         copy.wait()
 
 
-def copy_kernel(src, dst, sem):
-    copies = [
-        pltpu.make_async_copy(src.at[i, pl.ds(r, 16)], dst.at[i, pl.ds(r, 16)], sem.at[i, r // 16])
-        for i in range(src.shape[0])
-        for r in range(0, src.shape[1], 16)
-    ]
-    for copy in copies:
-        copy.start()
-    for copy in copies:
-        copy.wait()
+def copy_kernel(src, dst):
+    dst[...] = src[...]
 
 
 def per_device(pending, routes, probs, saved_gate, saved_up, w_gate, w_up, w_down, w_router):
@@ -270,6 +266,8 @@
             vmem((2, experts, cap, width), BF16),
             vmem((2, experts, cap, width), BF16),
             vmem((2, tokens, width), BF16),
+            vmem((2, tokens, width), BF16),
+            dma((2,)),
             dma((3,)),
             dma((2, chunks)),
             dma((2, chunks)), dma((2, chunks)),
@@ -289,10 +287,10 @@
     )
     result = pl.pallas_call(
         copy_kernel,
+        grid=(2, 2),
         out_shape=jax.ShapeDtypeStruct(result.shape, BF16),
-        in_specs=[any_spec],
-        out_specs=any_spec,
-        scratch_shapes=[dma((2, tokens // 16))],
+        in_specs=[pl.BlockSpec((1, tokens // 2, width), lambda i, j: (i, j, 0))],
+        out_specs=pl.BlockSpec((1, tokens // 2, width), lambda i, j: (i, j, 0)),
     )(result)
     return result[:, None]
 

time: 95.7 us -> 67.5 us (0.71)
  Pallas kernels: 95.6 us -> 67.3 us
    pallas_call x1, Pallas kernels: 29 us -> 3.32 us  [per_device(): pl.pallas_call(copy_kernel, grid=(2, 2), out_shape=jax.ShapeDtypeStruct(r...]
    pallas_call x1, Pallas kernels: 66.6 us -> 63.9 us  [per_device(): pl.pallas_call(functools.partial(layer_kernel, sections, experts, group,...]
where the time goes in v3:
time: 67.5 us; the launch traced here: 67.3 us
  Pallas kernels  67.3 us (100%)
    pallas_call x1, Pallas kernels, per_device(): pl.pallas_call(functools.partial(layer_kernel, sections, experts, group,...  63.9 us
    pallas_call x1, Pallas kernels, per_device(): pl.pallas_call(copy_kernel, grid=(2, 2), out_shape=jax.ShapeDtypeStruct(r...  3.32 us

profile of v3, /device:TPU:0, one launch (start us, length us, event | category | flops | bytes accessed | tf_op | source)
XLA Modules:
  0.0 67.3 jit_solution(12550662941849899619)
XLA Ops:
  0.0 63.9 %shard_map.91.src = bf16[2,64,3584]{2,1,0:T(8,128)(2,1)} custom-call(bf16[2,64,3584]{2,1,0:T(8,128)(2,1)} %bitcast.14, s32[2,64]{1,0:T(2,128)} %bitcast.21, bf16[2,64]{1,0:T(2,128)(2,1)} %bitcast.22, bf16[2,8,16,128]{3,2,1,0:T(8,128)(2,1)} %bitcast.18, bf16[2,8,16,128]{3,2,1,0:T(8,128)(2,1)} %bitcast.19, bf16[3584,128]{1,0:T(8,128)(2,1)} %bitcast.15, ...), custom_call_target="tpu_custom_call" | custom-call | flops 704643072 | bytes 8388608 | tf_op jit(solution)/shard_map/pallas_call | solution.py:251
  64.0 3.3 %shard_map.92 = bf16[2,64,3584]{2,1,0:T(8,128)(2,1)} custom-call(bf16[2,64,3584]{2,1,0:T(8,128)(2,1)} %shard_map.91.src), custom_call_target="tpu_custom_call" | custom-call | tf_op jit(solution)/shard_map/pallas_call | solution.py:288

commit v4 on v3

--- a/solution.py
+++ b/solution.py
@@ -11,6 +11,7 @@
 F32 = jnp.float32
 BF16 = jnp.bfloat16
 CHUNKS = 4
+SHARED = 2
 
 
 def dot(a, b, contract):
@@ -18,17 +19,21 @@
 
 
 def layer_kernel(
-    sections, experts, group, chunks,
+    sections, experts, group, chunks, shared,
     pend, routes, probs, gate, up, w_gate, w_up, w_down, router, out,
-    grad, wgu, wd, picked, rows, p_own, p_got, parts, halves, sums, home, done, held,
+    grad, wgu, wd, wall, z_out, z_got, picked, rows, p_own, p_got, parts, halves, sums, home, done, held,
     stage_sem, load_sem, out_sem, shift_send, shift_recv, p_send, p_recv, there_send, there_recv,
-    fwd_send, fwd_recv, red_send, red_recv, back_send, back_recv,
+    fwd_send, fwd_recv, w_send, w_recv, z_send, z_recv, red_send, red_recv, back_send, back_recv,
 ):
     members = experts * group
     tokens, width = grad.shape[1], grad.shape[2]
     cap = tokens // experts
     step = width // chunks
     cols = [pl.ds(c * step, step) for c in range(chunks)]
+    by_weights, by_rows = list(range(shared)), list(range(shared, chunks))
+    order = by_rows + by_weights
+    split = shared * step
+    hidden = w_gate.shape[1]
     sec, me = lax.axis_index("section"), lax.axis_index("expert")
     mine, side = me // group, me % group
     odd = sec % 2
@@ -47,7 +52,10 @@
         pltpu.make_async_copy(pend.at[1 - way[f]], held.at[f], stage_sem.at[f]) for f in range(2)
     ]
     loads = [
-        pltpu.make_async_copy(w_down, wd, load_sem.at[0]),
+        pltpu.make_async_copy(
+            w_down.at[:, pl.ds(0, split)], wall.at[side], load_sem.at[3]),
+        pltpu.make_async_copy(
+            w_down.at[:, pl.ds(split, width - split)], wd, load_sem.at[0]),
         pltpu.make_async_copy(w_gate, wgu.at[:, pl.ds(0, w_gate.shape[1])], load_sem.at[1]),
         pltpu.make_async_copy(
             w_up, wgu.at[:, pl.ds(w_gate.shape[1], w_up.shape[1])], load_sem.at[2]),
@@ -69,12 +77,23 @@
         return remote(held.at[f, :, cols[c]], grad.at[f, :, cols[c]],
                       shift_send.at[f, c], shift_recv.at[f, c], (source[f], me))
 
+    def start(copy):
+        copy.start()
+        sent.append(copy)
+
+    def share(c, m):
+        return remote(wall.at[side, :, cols[c]], wall.at[side, :, cols[c]],
+                      w_send.at[c, m], w_recv.at[c, m], at(mine, lax.rem(side + m, group)))
+
     for f in range(2):
         stage[f].wait()
-        for c in range(chunks):
-            copy = shift(f, c)
-            copy.start()
-            sent.append(copy)
+        for c in order:
+            start(shift(f, c))
+        if f == 0:
+            loads[0].wait()
+            for c in by_weights:
+                for m in range(1, group):
+                    start(share(c, m))
 
     table = []
     both_routes, both_probs = routes[...], probs[...].astype(F32)
@@ -127,9 +146,10 @@
         return remote(sums.at[f, to, :, cols[c]], home.at[f, mine, :, cols[c]],
                       back_send.at[f, c, k], back_recv.at[f, c, k], at(to, side))
 
-    def start(copy):
-        copy.start()
-        sent.append(copy)
+    def swap_z(f, m):
+        to = lax.rem(side + m, group)
+        return remote(z_out.at[f, to], z_got.at[f, side],
+                      z_send.at[f, m], z_recv.at[f, m], at(mine, to))
 
     def pick(f, c):
         shift(f, c).wait_recv()
@@ -137,8 +157,9 @@
         picked[f, :, :, cols[c]] = got.reshape(experts, cap, step)
         for k in range(experts - 1, 0, -1):
             start(there(f, c, k))
-        for m in range(1, group):
-            start(forward(f, c, 0, m))
+        if c in by_rows:
+            for m in range(1, group):
+                start(forward(f, c, 0, m))
         rows[f, mine, side, :, cols[c]] = picked[f, mine, :, cols[c]]
 
     def pass_on(f, c):
@@ -147,12 +168,36 @@
             for m in range(1, group):
                 start(forward(f, c, k, m))
 
-    def inner(f, c, z):
+    def beside(f):
+        total = jnp.zeros((tokens, group * hidden), F32)
+        for c in by_weights:
+            if f == 0:
+                for m in range(1, group):
+                    share(c, m).wait_recv()
+            for k in range(1, experts):
+                there(f, c, k).wait_recv()
+            own = rows[f, :, side, :, cols[c]].reshape(tokens, step)
+            weights = wall[:, :, cols[c]].reshape(group * hidden, step)
+            total = total + dot(own, weights, ((1,), (1,)))
+        for j in range(group):
+            z_out[f, j] = total[:, j * hidden:(j + 1) * hidden]
+        for m in range(1, group):
+            start(swap_z(f, m))
+        z_got[f, side] = z_out[f, side]
+
+    def inner(f, c):
         for k in range(experts):
             for m in range(1, group):
                 forward(f, c, k, m).wait_recv()
-        held = rows[f, :, :, :, cols[c]].reshape(members * cap, step)
-        return z + dot(held, wd[:, cols[c]], ((1,), (1,)))
+        held_rows = rows[f, :, :, :, cols[c]].reshape(members * cap, step)
+        weights = wd[:, pl.ds(c * step - split, step)]
+        return dot(held_rows, weights, ((1,), (1,)))
+
+    def all_z(f, z):
+        for m in range(1, group):
+            swap_z(f, m).wait_recv()
+        got = [z_got[f, j].reshape(experts, cap, hidden) for j in range(group)]
+        return z + jnp.stack(got, axis=1).reshape(members * cap, hidden)
 
     def middle(f, z):
         a = gate[way[f]].reshape(members * cap, -1).astype(F32)
@@ -163,12 +208,12 @@
         u = p * z
         grad_gate = (u * b * sg * (1.0 + a * (1.0 - sg))).astype(BF16)
         grad_up = (u * a * sg).astype(BF16)
-        hidden = jnp.concatenate([grad_gate, grad_up], axis=1)
-        return hidden, product * p * (1.0 - p)
-
-    def outer(f, c, hidden, scaled):
+        grads = jnp.concatenate([grad_gate, grad_up], axis=1)
+        return grads, product * p * (1.0 - p)
+
+    def outer(f, c, grads, scaled):
         column = router[pl.ds(mine, 1), cols[c]]
-        part = dot(hidden, wgu[cols[c], :], ((1,), (1,))) + scaled * column
+        part = dot(grads, wgu[cols[c], :], ((1,), (1,))) + scaled * column
         parts[f, :, :, :, cols[c]] = part.astype(BF16).reshape(experts, group, cap, step)
         for m in range(1, group):
             start(reduce(f, c, m))
@@ -194,34 +239,36 @@
         written.append(copy)
 
     written = []
-    for c in range(chunks):
+    for c in order:
         pick(0, c)
-    zero = jnp.zeros((members * cap, wd.shape[0]), F32)
-    loads[0].wait()
-    z = zero
-    for c in range(chunks):
-        pass_on(0, c)
+    for i, c in enumerate(order):
+        if c in by_rows:
+            pass_on(0, c)
         pick(1, c)
-        if c > 0:
-            z = inner(0, c - 1, z)
-    z = inner(0, chunks - 1, z)
+    for load in loads[1:]:
+        load.wait()
+    beside(0)
+    pass_on(1, by_rows[0])
+    z = jnp.zeros((members * cap, hidden), F32)
+    for c in by_rows:
+        z = z + inner(0, c)
     for k in range(1, members):
         p_copy(k).wait_recv()
-    hidden = middle(0, z)
-    for load in loads[1:]:
-        load.wait()
+    grads = middle(0, all_z(0, z))
     for c in range(chunks):
-        outer(0, c, *hidden)
-    z = zero
+        outer(0, c, *grads)
+    for c in by_rows[1:]:
+        pass_on(1, c)
+    beside(1)
+    add_up(0, 0)
+    z = jnp.zeros((members * cap, hidden), F32)
+    for c in by_rows:
+        z = z + inner(1, c)
+    grads = middle(1, all_z(1, z))
     for c in range(chunks):
-        pass_on(1, c)
+        outer(1, c, *grads)
+    for c in range(1, chunks):
         add_up(0, c)
-        if c > 0:
-            z = inner(1, c - 1, z)
-    z = inner(1, chunks - 1, z)
-    hidden = middle(1, z)
-    for c in range(chunks):
-        outer(1, c, *hidden)
     for c in range(chunks):
         finish(0, c)
         add_up(1, c)
@@ -233,10 +280,6 @@
         copy.wait()
 
 
-def copy_kernel(src, dst):
-    dst[...] = src[...]
-
-
 def per_device(pending, routes, probs, saved_gate, saved_up, w_gate, w_up, w_down, w_router):
     sections, members = lax.axis_size("section"), lax.axis_size("expert")
     experts = w_router.shape[2]
@@ -245,18 +288,22 @@
     cap = tokens // experts
     hidden = w_gate.shape[2]
     chunks = CHUNKS
+    split = SHARED * (width // chunks)
     dma, vmem = pltpu.SemaphoreType.DMA, pltpu.VMEM
     any_spec = pl.BlockSpec(memory_space=pl.ANY)
     vmem_spec = pl.BlockSpec(memory_space=pltpu.VMEM)
     result = pl.pallas_call(
-        functools.partial(layer_kernel, sections, experts, group, chunks),
+        functools.partial(layer_kernel, sections, experts, group, chunks, SHARED),
         out_shape=jax.ShapeDtypeStruct((2, tokens, width), BF16),
         in_specs=[any_spec] + [vmem_spec] * 4 + [any_spec] * 3 + [vmem_spec],
         out_specs=any_spec,
         scratch_shapes=[
             vmem((2, tokens, width), BF16),
             vmem((width, 2 * hidden), BF16),
-            vmem((hidden, width), BF16),
+            vmem((hidden, width - split), BF16),
+            vmem((group, hidden, split), BF16),
+            vmem((2, group, tokens, hidden), F32),
+            vmem((2, group, tokens, hidden), F32),
             vmem((2, experts, cap, width), BF16),
             vmem((2, experts, group, cap, width), BF16),
             vmem((experts, 2, cap, 128), BF16),
@@ -268,12 +315,14 @@
             vmem((2, tokens, width), BF16),
             vmem((2, tokens, width), BF16),
             dma((2,)),
-            dma((3,)),
+            dma((4,)),
             dma((2, chunks)),
             dma((2, chunks)), dma((2, chunks)),
             dma((members,)), dma((members,)),
             dma((2, chunks, experts)), dma((2, chunks, experts)),
             dma((2, chunks, experts, group)), dma((2, chunks, experts, group)),
+            dma((chunks, group)), dma((chunks, group)),
+            dma((2, group)), dma((2, group)),
             dma((2, chunks, group)), dma((2, chunks, group)),
             dma((2, chunks, experts)), dma((2, chunks, experts)),
         ],
@@ -285,13 +334,6 @@
         pending[:, 0], routes[:, 0, :, 0], probs[:, 0], saved_gate[:, 0, 0], saved_up[:, 0, 0],
         w_gate[0], w_up[0], w_down[0], jnp.transpose(w_router[0]),
     )
-    result = pl.pallas_call(
-        copy_kernel,
-        grid=(2, 2),
-        out_shape=jax.ShapeDtypeStruct(result.shape, BF16),
-        in_specs=[pl.BlockSpec((1, tokens // 2, width), lambda i, j: (i, j, 0))],
-        out_specs=pl.BlockSpec((1, tokens // 2, width), lambda i, j: (i, j, 0)),
-    )(result)
     return result[:, None]
 
 

time: 67.5 us -> 68.8 us (1.019)
  local copies, waits for them, and re-layouts: 0 us -> 2.16 us
  Pallas kernels: 67.3 us -> 66.4 us
    pallas_call x1 -> x0, Pallas kernels: 3.32 us -> none  [per_device(): pl.pallas_call(copy_kernel, grid=(2, 2), out_shape=jax.ShapeDtypeStruct(r...]
    pallas_call x1, Pallas kernels: 63.9 us -> 66.4 us  [per_device(): pl.pallas_call(functools.partial(layer_kernel, sections, experts, group,...]
    unnamed x0 -> x1, local copies, waits for them, and re-layouts: none -> 2.16 us
where the time goes in v4:
time: 68.8 us; the launch traced here: 68.6 us
  Pallas kernels  66.4 us (97%)
  local copies, waits for them, and re-layouts  2.16 us (3%)
    pallas_call x1, Pallas kernels, per_device(): pl.pallas_call(functools.partial(layer_kernel, sections, experts, group,...  66.4 us
    unnamed x1, local copies, waits for them, and re-layouts  2.16 us

profile of v4, /device:TPU:0, one launch (start us, length us, event | category | flops | bytes accessed | tf_op | source)
XLA Modules:
  0.0 68.6 jit_solution(11762394358308481007)
XLA Ops:
  0.0 66.4 %shard_map.91 = bf16[2,64,3584]{2,1,0:T(8,128)(2,1)} custom-call(bf16[2,64,3584]{2,1,0:T(8,128)(2,1)} %bitcast.15, s32[2,64]{1,0:T(2,128)} %bitcast.22, bf16[2,64]{1,0:T(2,128)(2,1)} %bitcast.23, bf16[2,8,16,128]{3,2,1,0:T(8,128)(2,1)} %bitcast.19, bf16[2,8,16,128]{3,2,1,0:T(8,128)(2,1)} %bitcast.20, bf16[3584,128]{1,0:T(8,128)(2,1)} %bitcast.16, ...), custom_call_target="tpu_custom_call" | custom-call | flops 704643072 | bytes 8388608 | tf_op jit(solution)/shard_map/pallas_call | solution.py:295
  66.4 2.2 %copy.12 = bf16[2,1,64,3584]{3,2,1,0:T(8,128)(2,1)} copy(bf16[2,1,64,3584]{3,2,1,0:T(8,128)(2,1)} %bitcast.14) | data formatting | bytes 1835008

commit v5 on v4

--- a/solution.py
+++ b/solution.py
@@ -259,16 +259,19 @@
         outer(0, c, *grads)
     for c in by_rows[1:]:
         pass_on(1, c)
+    add_up(0, 0)
     beside(1)
-    add_up(0, 0)
+    add_up(0, 1)
     z = jnp.zeros((members * cap, hidden), F32)
     for c in by_rows:
         z = z + inner(1, c)
+    add_up(0, 2)
     grads = middle(1, all_z(1, z))
     for c in range(chunks):
         outer(1, c, *grads)
-    for c in range(1, chunks):
-        add_up(0, c)
+        if c == 1:
+            for d in range(3, chunks):
+                add_up(0, d)
     for c in range(chunks):
         finish(0, c)
         add_up(1, c)

time: 68.8 us -> 64.9 us (0.943)
  Pallas kernels: 66.4 us -> 62.5 us
    pallas_call x1, Pallas kernels: 66.4 us -> 62.5 us  [per_device(): pl.pallas_call(functools.partial(layer_kernel, sections, experts, group,...]
where the time goes in v5:
time: 64.9 us; the launch traced here: 64.7 us
  Pallas kernels  62.5 us (96%)
  local copies, waits for them, and re-layouts  2.16 us (3%)
    pallas_call x1, Pallas kernels, per_device(): pl.pallas_call(functools.partial(layer_kernel, sections, experts, group,...  62.5 us
    unnamed x1, local copies, waits for them, and re-layouts  2.16 us

profile of v5, /device:TPU:0, one launch (start us, length us, event | category | flops | bytes accessed | tf_op | source)
XLA Modules:
  0.0 64.7 jit_solution(10628428546828466585)
XLA Ops:
  0.0 62.5 %shard_map.91 = bf16[2,64,3584]{2,1,0:T(8,128)(2,1)} custom-call(bf16[2,64,3584]{2,1,0:T(8,128)(2,1)} %bitcast.15, s32[2,64]{1,0:T(2,128)} %bitcast.22, bf16[2,64]{1,0:T(2,128)(2,1)} %bitcast.23, bf16[2,8,16,128]{3,2,1,0:T(8,128)(2,1)} %bitcast.19, bf16[2,8,16,128]{3,2,1,0:T(8,128)(2,1)} %bitcast.20, bf16[3584,128]{1,0:T(8,128)(2,1)} %bitcast.16, ...), custom_call_target="tpu_custom_call" | custom-call | flops 704643072 | bytes 8388608 | tf_op jit(solution)/shard_map/pallas_call | solution.py:298
  62.6 2.2 %copy.12 = bf16[2,1,64,3584]{3,2,1,0:T(8,128)(2,1)} copy(bf16[2,1,64,3584]{3,2,1,0:T(8,128)(2,1)} %bitcast.14) | data formatting | bytes 1835008

commit v6 on v5

--- a/solution.py
+++ b/solution.py
@@ -2,6 +2,7 @@
 
 import jax
 import jax.numpy as jnp
+import numpy as np
 from jax import lax
 from jax.experimental import pallas as pl
 from jax.experimental.pallas import tpu as pltpu
@@ -10,8 +11,9 @@
 MESH = pl.DeviceIdType.MESH
 F32 = jnp.float32
 BF16 = jnp.bfloat16
-CHUNKS = 4
-SHARED = 2
+IN_CUT = (7, 5, 8, 8)
+OUT_CUT = ((7, 7, 7, 7), (8, 8, 6, 4, 2))
+SHARED = 1
 
 
 def dot(a, b, contract):
@@ -19,7 +21,7 @@
 
 
 def layer_kernel(
-    sections, experts, group, chunks, shared,
+    sections, experts, group,
     pend, routes, probs, gate, up, w_gate, w_up, w_down, router, out,
     grad, wgu, wd, wall, z_out, z_got, picked, rows, p_own, p_got, parts, halves, sums, home, done, held,
     stage_sem, load_sem, out_sem, shift_send, shift_recv, p_send, p_recv, there_send, there_recv,
@@ -28,11 +30,15 @@
     members = experts * group
     tokens, width = grad.shape[1], grad.shape[2]
     cap = tokens // experts
-    step = width // chunks
-    cols = [pl.ds(c * step, step) for c in range(chunks)]
-    by_weights, by_rows = list(range(shared)), list(range(shared, chunks))
+    unit = width // sum(IN_CUT)
+
+    def spans(cut):
+        return [pl.ds(sum(cut[:c]) * unit, cut[c] * unit) for c in range(len(cut))]
+
+    cols, ocols = spans(IN_CUT), [spans(cut) for cut in OUT_CUT]
+    by_weights, by_rows = list(range(SHARED)), list(range(SHARED, len(cols)))
     order = by_rows + by_weights
-    split = shared * step
+    split = sum(IN_CUT[:SHARED]) * unit
     hidden = w_gate.shape[1]
     sec, me = lax.axis_index("section"), lax.axis_index("expert")
     mine, side = me // group, me % group
@@ -138,12 +144,12 @@
 
     def reduce(f, c, m):
         to = lax.rem(side + m, group)
-        return remote(parts.at[f, :, to, :, cols[c]], halves.at[f, m - 1, :, :, cols[c]],
+        return remote(parts.at[f, :, to, :, ocols[f][c]], halves.at[f, m - 1, :, :, ocols[f][c]],
                       red_send.at[f, c, m], red_recv.at[f, c, m], at(mine, to))
 
     def back(f, c, k):
         to = lax.rem(mine + k, experts)
-        return remote(sums.at[f, to, :, cols[c]], home.at[f, mine, :, cols[c]],
+        return remote(sums.at[f, to, :, ocols[f][c]], home.at[f, mine, :, ocols[f][c]],
                       back_send.at[f, c, k], back_recv.at[f, c, k], at(to, side))
 
     def swap_z(f, m):
@@ -154,7 +160,7 @@
     def pick(f, c):
         shift(f, c).wait_recv()
         got = dot(table[f], grad[f, :, cols[c]], ((1,), (0,))).astype(BF16)
-        picked[f, :, :, cols[c]] = got.reshape(experts, cap, step)
+        picked[f, :, :, cols[c]] = got.reshape(experts, cap, cols[c].size)
         for k in range(experts - 1, 0, -1):
             start(there(f, c, k))
         if c in by_rows:
@@ -176,8 +182,8 @@
                     share(c, m).wait_recv()
             for k in range(1, experts):
                 there(f, c, k).wait_recv()
-            own = rows[f, :, side, :, cols[c]].reshape(tokens, step)
-            weights = wall[:, :, cols[c]].reshape(group * hidden, step)
+            own = rows[f, :, side, :, cols[c]].reshape(tokens, cols[c].size)
+            weights = wall[:, :, cols[c]].reshape(group * hidden, cols[c].size)
             total = total + dot(own, weights, ((1,), (1,)))
         for j in range(group):
             z_out[f, j] = total[:, j * hidden:(j + 1) * hidden]
@@ -189,8 +195,8 @@
         for k in range(experts):
             for m in range(1, group):
                 forward(f, c, k, m).wait_recv()
-        held_rows = rows[f, :, :, :, cols[c]].reshape(members * cap, step)
-        weights = wd[:, pl.ds(c * step - split, step)]
+        held_rows = rows[f, :, :, :, cols[c]].reshape(members * cap, cols[c].size)
+        weights = wd[:, pl.ds(cols[c].start - split, cols[c].size)]
         return dot(held_rows, weights, ((1,), (1,)))
 
     def all_z(f, z):
@@ -212,36 +218,37 @@
         return grads, product * p * (1.0 - p)
 
     def outer(f, c, grads, scaled):
-        column = router[pl.ds(mine, 1), cols[c]]
-        part = dot(grads, wgu[cols[c], :], ((1,), (1,))) + scaled * column
-        parts[f, :, :, :, cols[c]] = part.astype(BF16).reshape(experts, group, cap, step)
+        column = router[pl.ds(mine, 1), ocols[f][c]]
+        part = dot(grads, wgu[ocols[f][c], :], ((1,), (1,))) + scaled * column
+        parts[f, :, :, :, ocols[f][c]] = part.astype(BF16).reshape(experts, group, cap, ocols[f][c].size)
         for m in range(1, group):
             start(reduce(f, c, m))
 
     def add_up(f, c):
-        total = parts[f, :, side, :, cols[c]].astype(F32)
+        total = parts[f, :, side, :, ocols[f][c]].astype(F32)
         for m in range(1, group):
             reduce(f, c, m).wait_recv()
-            total = total + halves[f, m - 1, :, :, cols[c]].astype(F32)
-        sums[f, :, :, cols[c]] = total.astype(BF16)
+            total = total + halves[f, m - 1, :, :, ocols[f][c]].astype(F32)
+        sums[f, :, :, ocols[f][c]] = total.astype(BF16)
         for k in range(experts - 1, 0, -1):
             start(back(f, c, k))
-        home[f, mine, :, cols[c]] = sums[f, mine, :, cols[c]]
+        home[f, mine, :, ocols[f][c]] = sums[f, mine, :, ocols[f][c]]
 
     def finish(f, c):
         for k in range(1, experts):
             back(f, c, k).wait_recv()
-        got = dot(table[f], home[f, :, :, cols[c]].reshape(tokens, step), ((0,), (0,)))
-        done[f, :, cols[c]] = (grad[f, :, cols[c]].astype(F32) + got).astype(BF16)
+        got = dot(table[f], home[f, :, :, ocols[f][c]].reshape(tokens, ocols[f][c].size), ((0,), (0,)))
+        done[f, :, ocols[f][c]] = (grad[f, :, ocols[f][c]].astype(F32) + got).astype(BF16)
         copy = pltpu.make_async_copy(
-            done.at[f, :, cols[c]], out.at[way[f], :, cols[c]], out_sem.at[f, c])
+            done.at[f, :, ocols[f][c]], out.at[way[f], :, ocols[f][c]], out_sem.at[f, c])
         copy.start()
         written.append(copy)
 
     written = []
+    last = [len(o) for o in ocols]
     for c in order:
         pick(0, c)
-    for i, c in enumerate(order):
+    for c in order:
         if c in by_rows:
             pass_on(0, c)
         pick(1, c)
@@ -255,7 +262,7 @@
     for k in range(1, members):
         p_copy(k).wait_recv()
     grads = middle(0, all_z(0, z))
-    for c in range(chunks):
+    for c in range(last[0]):
         outer(0, c, *grads)
     for c in by_rows[1:]:
         pass_on(1, c)
@@ -267,15 +274,17 @@
         z = z + inner(1, c)
     add_up(0, 2)
     grads = middle(1, all_z(1, z))
-    for c in range(chunks):
+    for c in range(last[1]):
         outer(1, c, *grads)
         if c == 1:
-            for d in range(3, chunks):
+            for d in range(3, last[0]):
                 add_up(0, d)
-    for c in range(chunks):
+    for c in range(last[0]):
         finish(0, c)
         add_up(1, c)
-    for c in range(chunks):
+    for c in range(last[0], last[1]):
+        add_up(1, c)
+    for c in range(last[1]):
         finish(1, c)
     for copy in sent:
         copy.wait_send()
@@ -290,47 +299,50 @@
     tokens, width = pending.shape[2], pending.shape[3]
     cap = tokens // experts
     hidden = w_gate.shape[2]
-    chunks = CHUNKS
-    split = SHARED * (width // chunks)
+    chunks, pieces = len(IN_CUT), max(len(cut) for cut in OUT_CUT)
+    split = sum(IN_CUT[:SHARED]) * (width // sum(IN_CUT))
     dma, vmem = pltpu.SemaphoreType.DMA, pltpu.VMEM
     any_spec = pl.BlockSpec(memory_space=pl.ANY)
     vmem_spec = pl.BlockSpec(memory_space=pltpu.VMEM)
+    scratch = [
+        vmem((2, tokens, width), BF16),
+        vmem((width, 2 * hidden), BF16),
+        vmem((hidden, width - split), BF16),
+        vmem((group, hidden, split), BF16),
+        vmem((2, group, tokens, hidden), F32),
+        vmem((2, group, tokens, hidden), F32),
+        vmem((2, experts, cap, width), BF16),
+        vmem((2, experts, group, cap, width), BF16),
+        vmem((experts, 2, cap, 128), BF16),
+        vmem((members, 2, cap, 128), BF16),
+        vmem((2, experts, group, cap, width), BF16),
+        vmem((2, max(group - 1, 1), experts, cap, width), BF16),
+        vmem((2, experts, cap, width), BF16),
+        vmem((2, experts, cap, width), BF16),
+        vmem((2, tokens, width), BF16),
+        vmem((2, tokens, width), BF16),
+        dma((2,)),
+        dma((4,)),
+        dma((2, pieces)),
+        dma((2, chunks)), dma((2, chunks)),
+        dma((members,)), dma((members,)),
+        dma((2, chunks, experts)), dma((2, chunks, experts)),
+        dma((2, chunks, experts, group)), dma((2, chunks, experts, group)),
+        dma((chunks, group)), dma((chunks, group)),
+        dma((2, group)), dma((2, group)),
+        dma((2, pieces, group)), dma((2, pieces, group)),
+        dma((2, pieces, experts)), dma((2, pieces, experts)),
+    ]
+    room = sum(
+        int(np.prod(s.shape)) * s.dtype.itemsize for s in scratch if s.memory_space == pltpu.VMEM)
     result = pl.pallas_call(
-        functools.partial(layer_kernel, sections, experts, group, chunks, SHARED),
+        functools.partial(layer_kernel, sections, experts, group),
         out_shape=jax.ShapeDtypeStruct((2, tokens, width), BF16),
         in_specs=[any_spec] + [vmem_spec] * 4 + [any_spec] * 3 + [vmem_spec],
         out_specs=any_spec,
-        scratch_shapes=[
-            vmem((2, tokens, width), BF16),
-            vmem((width, 2 * hidden), BF16),
-            vmem((hidden, width - split), BF16),
-            vmem((group, hidden, split), BF16),
-            vmem((2, group, tokens, hidden), F32),
-            vmem((2, group, tokens, hidden), F32),
-            vmem((2, experts, cap, width), BF16),
-            vmem((2, experts, group, cap, width), BF16),
-            vmem((experts, 2, cap, 128), BF16),
-            vmem((members, 2, cap, 128), BF16),
-            vmem((2, experts, group, cap, width), BF16),
-            vmem((2, max(group - 1, 1), experts, cap, width), BF16),
-            vmem((2, experts, cap, width), BF16),
-            vmem((2, experts, cap, width), BF16),
-            vmem((2, tokens, width), BF16),
-            vmem((2, tokens, width), BF16),
-            dma((2,)),
-            dma((4,)),
-            dma((2, chunks)),
-            dma((2, chunks)), dma((2, chunks)),
-            dma((members,)), dma((members,)),
-            dma((2, chunks, experts)), dma((2, chunks, experts)),
-            dma((2, chunks, experts, group)), dma((2, chunks, experts, group)),
-            dma((chunks, group)), dma((chunks, group)),
-            dma((2, group)), dma((2, group)),
-            dma((2, chunks, group)), dma((2, chunks, group)),
-            dma((2, chunks, experts)), dma((2, chunks, experts)),
-        ],
+        scratch_shapes=scratch,
         compiler_params=pltpu.CompilerParams(
-            collective_id=0, has_side_effects=True, vmem_limit_bytes=56 << 20),
+            collective_id=0, has_side_effects=True, vmem_limit_bytes=room + (8 << 20)),
         cost_estimate=pl.CostEstimate(
             flops=12 * members * cap * hidden * width, bytes_accessed=8 << 20, transcendentals=0),
     )(

time: 64.9 us -> 71.5 us (1.10)
  local copies, waits for them, and re-layouts: 2.16 us -> 8.82 us
    unnamed x1 -> x19, local copies, waits for them, and re-layouts: 2.16 us -> 8.82 us
where the time goes in v6:
time: 71.5 us; the launch traced here: 71.1 us
  Pallas kernels  62.3 us (87%)
  local copies, waits for them, and re-layouts  8.82 us (12%)
    pallas_call x1, Pallas kernels, per_device(): pl.pallas_call(functools.partial(layer_kernel, sections, experts, group),...  62.3 us
    unnamed x19, local copies, waits for them, and re-layouts  8.82 us

profile of v6, /device:TPU:0, one launch (start us, length us, event | category | flops | bytes accessed | tf_op | source)
XLA Modules:
  0.0 71.1 jit_solution(5440973185667343520)
XLA Ops:
  0.0 0.0 copy-start.7
  0.0 0.0 copy-start.8
  0.0 0.7 copy-done.7
  0.7 0.0 copy-done.8
  0.7 0.0 copy-start
  0.7 1.2 %copy-done = bf16[2,1,64,3584]{3,2,1,0:T(8,128)(2,1)S(1)} copy-done((bf16[2,1,64,3584]{3,2,1,0:T(8,128)(2,1)S(1)}, bf16[2,1,64,3584]{3,2,1,0:T(8,128)(2,1)}, u32[]{:S(2)}) %copy-start) | copy-done | bytes 917528
  1.9 0.0 copy-start.1
  1.9 1.2 %copy-done.1 = bf16[1,3584,128]{2,1,0:T(8,128)(2,1)S(1)} copy-done((bf16[1,3584,128]{2,1,0:T(8,128)(2,1)S(1)}, bf16[1,3584,128]{2,1,0:T(8,128)(2,1)}, u32[]{:S(2)}) %copy-start.1) | copy-done | bytes 917528
  3.0 0.0 copy-start.2
  3.0 1.2 %copy-done.2 = bf16[1,3584,128]{2,1,0:T(8,128)(2,1)S(1)} copy-done((bf16[1,3584,128]{2,1,0:T(8,128)(2,1)S(1)}, bf16[1,3584,128]{2,1,0:T(8,128)(2,1)}, u32[]{:S(2)}) %copy-start.2) | copy-done | bytes 917528
  4.2 0.0 copy-start.3
  4.2 1.2 %copy-done.3 = bf16[1,128,3584]{2,1,0:T(8,128)(2,1)S(1)} copy-done((bf16[1,128,3584]{2,1,0:T(8,128)(2,1)S(1)}, bf16[1,128,3584]{2,1,0:T(8,128)(2,1)}, u32[]{:S(2)}) %copy-start.3) | copy-done | bytes 917528
  5.4 0.0 copy-start.4
  5.4 0.8 %copy-done.4 = bf16[2,1,1,8,16,128]{5,4,3,2,1,0:T(8,128)(2,1)S(1)} copy-done((bf16[2,1,1,8,16,128]{5,4,3,2,1,0:T(8,128)(2,1)S(1)}, bf16[2,1,1,8,16,128]{5,4,3,2,1,0:T(8,128)(2,1)}, u32[]{:S(2)}) %copy-start.4) | copy-done | bytes 65560
  6.2 0.0 copy-start.5
  6.2 0.8 %copy-done.5 = bf16[2,1,1,8,16,128]{5,4,3,2,1,0:T(8,128)(2,1)S(1)} copy-done((bf16[2,1,1,8,16,128]{5,4,3,2,1,0:T(8,128)(2,1)S(1)}, bf16[2,1,1,8,16,128]{5,4,3,2,1,0:T(8,128)(2,1)}, u32[]{:S(2)}) %copy-start.5) | copy-done | bytes 65560
  7.1 0.0 copy-start.6
  7.1 0.8 %copy-done.6 = f32[1,3584,4]{1,2,0:T(4,128)S(1)} copy-done((f32[1,3584,4]{1,2,0:T(4,128)S(1)}, f32[1,3584,4]{1,2,0:T(4,128)}, u32[]{:S(2)}) %copy-start.6) | copy-done | bytes 57368
  7.9 62.3 %shard_map.91 = bf16[2,64,3584]{2,1,0:T(8,128)(2,1)S(1)} custom-call(bf16[2,64,3584]{2,1,0:T(8,128)(2,1)S(1)} %bitcast.15, s32[2,64]{1,0:T(2,128)S(1)} %bitcast.22, bf16[2,64]{1,0:T(2,128)(2,1)S(1)} %bitcast.23, bf16[2,8,16,128]{3,2,1,0:T(8,128)(2,1)S(1)} %bitcast.19, bf16[2,8,16,128]{3,2,1,0:T(8,128)(2,1)S(1)} %bitcast.20, bf16[3584,128]{1,0:T(8,128)(2,1)S(1)} %bitcast.16, ...), custom_call_target="tpu_custom_call" | custom-call | flops 704643072 | bytes 8388608 | tf_op jit(solution)/shard_map/pallas_call | solution.py:338
  70.2 0.9 %copy.12 = bf16[2,1,64,3584]{3,2,1,0:T(8,128)(2,1)} copy(bf16[2,1,64,3584]{3,2,1,0:T(8,128)(2,1)S(1)} %bitcast.14) | data formatting | bytes 1835008
Async XLA Ops:
  0.0 0.7 copy-start.7
  0.0 0.7 copy-start.8
  0.7 1.2 %copy-start = (bf16[2,1,64,3584]{3,2,1,0:T(8,128)(2,1)S(1)}, bf16[2,1,64,3584]{3,2,1,0:T(8,128)(2,1)}, u32[]{:S(2)}) copy-start(bf16[2,1,64,3584]{3,2,1,0:T(8,128)(2,1)} %param.9) | copy-start | bytes 2752516
  1.9 1.2 %copy-start.1 = (bf16[1,3584,128]{2,1,0:T(8,128)(2,1)S(1)}, bf16[1,3584,128]{2,1,0:T(8,128)(2,1)}, u32[]{:S(2)}) copy-start(bf16[1,3584,128]{2,1,0:T(8,128)(2,1)} %param.14) | copy-start | bytes 2752516
  3.0 1.2 %copy-start.2 = (bf16[1,3584,128]{2,1,0:T(8,128)(2,1)S(1)}, bf16[1,3584,128]{2,1,0:T(8,128)(2,1)}, u32[]{:S(2)}) copy-start(bf16[1,3584,128]{2,1,0:T(8,128)(2,1)} %param.15) | copy-start | bytes 2752516
  4.2 1.2 %copy-start.3 = (bf16[1,128,3584]{2,1,0:T(8,128)(2,1)S(1)}, bf16[1,128,3584]{2,1,0:T(8,128)(2,1)}, u32[]{:S(2)}) copy-start(bf16[1,128,3584]{2,1,0:T(8,128)(2,1)} %param.16) | copy-start | bytes 2752516
  5.4 0.8 %copy-start.4 = (bf16[2,1,1,8,16,128]{5,4,3,2,1,0:T(8,128)(2,1)S(1)}, bf16[2,1,1,8,16,128]{5,4,3,2,1,0:T(8,128)(2,1)}, u32[]{:S(2)}) copy-start(bf16[2,1,1,8,16,128]{5,4,3,2,1,0:T(8,128)(2,1)} %param.12) | copy-start | bytes 196612
  6.2 0.8 %copy-start.5 = (bf16[2,1,1,8,16,128]{5,4,3,2,1,0:T(8,128)(2,1)S(1)}, bf16[2,1,1,8,16,128]{5,4,3,2,1,0:T(8,128)(2,1)}, u32[]{:S(2)}) copy-start(bf16[2,1,1,8,16,128]{5,4,3,2,1,0:T(8,128)(2,1)} %param.13) | copy-start | bytes 196612
  7.1 0.8 %copy-start.6 = (f32[1,3584,4]{1,2,0:T(4,128)S(1)}, f32[1,3584,4]{1,2,0:T(4,128)}, u32[]{:S(2)}) copy-start(f32[1,3584,4]{1,2,0:T(4,128)} %param.17) | copy-start | bytes 172036

commit v7 on v6

--- a/solution.py
+++ b/solution.py
@@ -22,9 +22,10 @@
 
 def layer_kernel(
     sections, experts, group,
-    pend, routes, probs, gate, up, w_gate, w_up, w_down, router, out,
+    pend, routes_in, probs_in, gate_in, up_in, w_gate, w_up, w_down, router_in, out,
+    routes, probs, gate, up, router,
     grad, wgu, wd, wall, z_out, z_got, picked, rows, p_own, p_got, parts, halves, sums, home, done, held,
-    stage_sem, load_sem, out_sem, shift_send, shift_recv, p_send, p_recv, there_send, there_recv,
+    stage_sem, load_sem, small_sem, out_sem, shift_send, shift_recv, p_send, p_recv, there_send, there_recv,
     fwd_send, fwd_recv, w_send, w_recv, z_send, z_recv, red_send, red_recv, back_send, back_recv,
 ):
     members = experts * group
@@ -66,7 +67,13 @@
         pltpu.make_async_copy(
             w_up, wgu.at[:, pl.ds(w_gate.shape[1], w_up.shape[1])], load_sem.at[2]),
     ]
-    for load in stage + loads:
+    small = [
+        pltpu.make_async_copy(src, dst, small_sem.at[i])
+        for i, (src, dst) in enumerate((
+            (routes_in, routes), (probs_in, probs), (gate_in, gate), (up_in, up),
+            (router_in, router)))
+    ]
+    for load in stage + loads[:1] + small + loads[1:]:
         load.start()
 
     barrier = pltpu.get_barrier_semaphore()
@@ -102,6 +109,8 @@
                     start(share(c, m))
 
     table = []
+    for load in small[:2]:
+        load.wait()
     both_routes, both_probs = routes[...], probs[...].astype(F32)
     before = (lax.broadcasted_iota(jnp.int32, (tokens, tokens), 0)
               < lax.broadcasted_iota(jnp.int32, (tokens, tokens), 1)).astype(F32)
@@ -252,7 +261,7 @@
         if c in by_rows:
             pass_on(0, c)
         pick(1, c)
-    for load in loads[1:]:
+    for load in loads[1:] + small[2:]:
         load.wait()
     beside(0)
     pass_on(1, by_rows[0])
@@ -303,8 +312,12 @@
     split = sum(IN_CUT[:SHARED]) * (width // sum(IN_CUT))
     dma, vmem = pltpu.SemaphoreType.DMA, pltpu.VMEM
     any_spec = pl.BlockSpec(memory_space=pl.ANY)
-    vmem_spec = pl.BlockSpec(memory_space=pltpu.VMEM)
     scratch = [
+        vmem((2, tokens), jnp.int32),
+        vmem((2, tokens), BF16),
+        vmem((2, members, cap, hidden), BF16),
+        vmem((2, members, cap, hidden), BF16),
+        vmem((experts, width), F32),
         vmem((2, tokens, width), BF16),
         vmem((width, 2 * hidden), BF16),
         vmem((hidden, width - split), BF16),
@@ -323,6 +336,7 @@
         vmem((2, tokens, width), BF16),
         dma((2,)),
         dma((4,)),
+        dma((5,)),
         dma((2, pieces)),
         dma((2, chunks)), dma((2, chunks)),
         dma((members,)), dma((members,)),
@@ -338,17 +352,17 @@
     result = pl.pallas_call(
         functools.partial(layer_kernel, sections, experts, group),
         out_shape=jax.ShapeDtypeStruct((2, tokens, width), BF16),
-        in_specs=[any_spec] + [vmem_spec] * 4 + [any_spec] * 3 + [vmem_spec],
+        in_specs=[pl.BlockSpec(memory_space=pltpu.HBM)] * 9,
         out_specs=any_spec,
         scratch_shapes=scratch,
         compiler_params=pltpu.CompilerParams(
             collective_id=0, has_side_effects=True, vmem_limit_bytes=room + (8 << 20)),
         cost_estimate=pl.CostEstimate(
             flops=12 * members * cap * hidden * width, bytes_accessed=8 << 20, transcendentals=0),
-    )(
+    )(*[pltpu.with_memory_space_constraint(value, pltpu.HBM) for value in (
         pending[:, 0], routes[:, 0, :, 0], probs[:, 0], saved_gate[:, 0, 0], saved_up[:, 0, 0],
         w_gate[0], w_up[0], w_down[0], jnp.transpose(w_router[0]),
-    )
+    )])
     return result[:, None]
 
 

time: 71.5 us -> 63.3 us (0.89)
  local copies, waits for them, and re-layouts: 8.82 us -> 0.93 us
    unnamed x19 -> x1, local copies, waits for them, and re-layouts: 8.82 us -> 0.93 us
where the time goes in v7:
time: 63.3 us; the launch traced here: 63.2 us
  Pallas kernels  62.2 us (98%)
  local copies, waits for them, and re-layouts  0.93 us (1%)
    pallas_call x1, Pallas kernels, per_device(): pl.pallas_call(functools.partial(layer_kernel, sections, experts, group),...  62.2 us

profile of v7, /device:TPU:0, one launch (start us, length us, event | category | flops | bytes accessed | tf_op | source)
XLA Modules:
  0.0 63.2 jit_solution(2483512015809098499)
XLA Ops:
  0.0 62.2 %shard_map.91 = bf16[2,64,3584]{2,1,0:T(8,128)(2,1)S(1)} custom-call(bf16[2,64,3584]{2,1,0:T(8,128)(2,1)} %bitcast.15, s32[2,64]{1,0:T(2,128)} %bitcast.22, bf16[2,64]{1,0:T(2,128)(2,1)} %bitcast.23, bf16[2,8,16,128]{3,2,1,0:T(8,128)(2,1)} %bitcast.19, bf16[2,8,16,128]{3,2,1,0:T(8,128)(2,1)} %bitcast.20, bf16[3584,128]{1,0:T(8,128)(2,1)} %bitcast.16, ...), custom_call_target="tpu_custom_call" | custom-call | flops 704643072 | bytes 8388608 | tf_op jit(solution)/shard_map/pallas_call | solution.py:352
  62.3 0.9 %copy.12 = bf16[2,1,64,3584]{3,2,1,0:T(8,128)(2,1)} copy(bf16[2,1,64,3584]{3,2,1,0:T(8,128)(2,1)S(1)} %bitcast.14) | data formatting | bytes 1835008

commit v8 on v7

--- a/solution.py
+++ b/solution.py
@@ -271,12 +271,14 @@
     for k in range(1, members):
         p_copy(k).wait_recv()
     grads = middle(0, all_z(0, z))
-    for c in range(last[0]):
-        outer(0, c, *grads)
-    for c in by_rows[1:]:
-        pass_on(1, c)
+    outer(0, 0, *grads)
+    pass_on(1, by_rows[1])
+    outer(0, 1, *grads)
+    pass_on(1, by_rows[2])
+    outer(0, 2, *grads)
     add_up(0, 0)
     beside(1)
+    outer(0, 3, *grads)
     add_up(0, 1)
     z = jnp.zeros((members * cap, hidden), F32)
     for c in by_rows:

time: 63.3 us -> 61.8 us (0.976)
  Pallas kernels: 62.2 us -> 60.7 us
    pallas_call x1, Pallas kernels: 62.2 us -> 60.7 us  [per_device(): pl.pallas_call(functools.partial(layer_kernel, sections, experts, group),...]
where the time goes in v8:
time: 61.8 us; the launch traced here: 61.7 us
  Pallas kernels  60.7 us (98%)
  local copies, waits for them, and re-layouts  0.93 us (2%)
    pallas_call x1, Pallas kernels, per_device(): pl.pallas_call(functools.partial(layer_kernel, sections, experts, group),...  60.7 us

profile of v8, /device:TPU:0, one launch (start us, length us, event | category | flops | bytes accessed | tf_op | source)
XLA Modules:
  0.0 61.7 jit_solution(12187948330144899326)
XLA Ops:
  0.0 60.7 %shard_map.91 = bf16[2,64,3584]{2,1,0:T(8,128)(2,1)S(1)} custom-call(bf16[2,64,3584]{2,1,0:T(8,128)(2,1)} %bitcast.15, s32[2,64]{1,0:T(2,128)} %bitcast.22, bf16[2,64]{1,0:T(2,128)(2,1)} %bitcast.23, bf16[2,8,16,128]{3,2,1,0:T(8,128)(2,1)} %bitcast.19, bf16[2,8,16,128]{3,2,1,0:T(8,128)(2,1)} %bitcast.20, bf16[3584,128]{1,0:T(8,128)(2,1)} %bitcast.16, ...), custom_call_target="tpu_custom_call" | custom-call | flops 704643072 | bytes 8388608 | tf_op jit(solution)/shard_map/pallas_call | solution.py:354
  60.7 0.9 %copy.12 = bf16[2,1,64,3584]{3,2,1,0:T(8,128)(2,1)} copy(bf16[2,1,64,3584]{3,2,1,0:T(8,128)(2,1)S(1)} %bitcast.14) | data formatting | bytes 1835008
